TPU v7x, 512 devices: a whole 4x8x8 slice. The times are simulated.
512 devices in a mesh: slab: 64 (over z_hi, y, core), coil: 8 (over z_lo, x).
Axes of the slice: x: 4, y: 8, z: 8 (z_hi: 4, z_lo: 2; z = z_hi * 2 + z_lo), core: 2. Of those that a mesh axis runs over, the one named last changes fastest.
Arguments:
- image: float32 [64, 32, 2, 320], P('slab', 'coil'), may hold values from -6 to 6
- sampled_lines: int32 [64, 80], P('slab'), may hold values from 0 to 319, as said below
- coil_maps: float32 [32, 64, 32, 2, 320], P('coil', 'slab'), may hold values from -2 to 2
- kspace: float32 [32, 64, 32, 2, 320], P('coil', 'slab'), may hold values from -16 to 16
- reg_weight: float32 [1], replicated, may hold values from 0.05 to 0.5
- conv_first: bfloat16 [3, 3, 3, 2, 64], replicated, may hold values from -1.25 to 1.25
- conv_middle: bfloat16 [2, 3, 3, 3, 64, 64], replicated, may hold values from -0.21875 to 0.21875
- conv_last: bfloat16 [3, 3, 3, 64, 2], replicated, may hold values from -0.15625 to 0.15625
Outputs:
- denoised: float32 [64, 32, 2, 320], P('slab', 'coil')
- reconstruction: float32 [64, 32, 2, 320], P('slab', 'coil')
Inputs may be any that keep to these rules, and one draw needn't show every extreme that they name: `sampled_lines`: each row holds 80 different line indices; among them are the 24 lines starting at 148 and the lines 0 and 319.
All inputs are finite; a program needn't handle non-finite values.
Results may differ from a plain program's by a relative error of at most 0.0059.
Values may be sent and summed in bfloat16 or wider, within the bound.
A program may use at most 64 MiB of HBM per device.

v0:
```python
import math

import jax
import jax.numpy as jnp
from jax import lax
from jax.sharding import PartitionSpec as P

ITERS = 4


def padded_2(block, sides, width):
    for axis, dim in sides:
        count = lax.axis_size(axis)
        forward = [(i, i + 1) for i in range(count - 1)]
        backward = [(target, source) for source, target in forward]
        low = lax.ppermute(
            lax.slice_in_dim(block, block.shape[dim] - width, None, axis=dim), axis, forward
        )
        high = lax.ppermute(lax.slice_in_dim(block, 0, width, axis=dim), axis, backward)
        block = jnp.concatenate([low, block, high], axis=dim)
    return block


def complex_product(first_factor, second_factor):
    real_part = (
        first_factor[..., 0, :] * second_factor[..., 0, :]
        - first_factor[..., 1, :] * second_factor[..., 1, :]
    )
    imag_part = (
        first_factor[..., 0, :] * second_factor[..., 1, :]
        + first_factor[..., 1, :] * second_factor[..., 0, :]
    )
    return jnp.stack([real_part, imag_part], axis=-2)


def conjugate_product(first_factor, second_factor):
    real_part = (
        first_factor[..., 0, :] * second_factor[..., 0, :]
        + first_factor[..., 1, :] * second_factor[..., 1, :]
    )
    imag_part = (
        first_factor[..., 0, :] * second_factor[..., 1, :]
        - first_factor[..., 1, :] * second_factor[..., 0, :]
    )
    return jnp.stack([real_part, imag_part], axis=-2)


def window_product(padded, weight, slab_rows, line_count, point_count):
    summed = None
    for shift_z in range(3):
        columns = jnp.concatenate(
            [
                padded[
                    shift_z : shift_z + slab_rows,
                    shift_x : shift_x + line_count,
                    shift_y : shift_y + point_count,
                    :,
                ]
                for shift_x in range(3)
                for shift_y in range(3)
            ],
            axis=-1,
        )
        kernel = weight[shift_z].reshape(-1, weight.shape[-1])
        contribution = jnp.einsum(
            "abcd,de->abce", columns, kernel, preferred_element_type=jnp.float32
        )
        summed = contribution if summed is None else summed + contribution
    return summed


def convolve_slabs(activation, weight):
    padded = padded_2(activation, (("slab", 0), ("coil", 1)), 1)
    padded = jnp.pad(padded, ((0, 0), (0, 0), (1, 1), (0, 0)))
    return window_product(
        padded, weight, activation.shape[0], activation.shape[1], activation.shape[2]
    )


def transform_tables(points):
    positions = jnp.arange(points, dtype=jnp.int32)
    phase_steps = positions[:, None] * positions[None, :] % points
    angles = phase_steps.astype(jnp.float32) * (2.0 * math.pi / points)
    cosine = jnp.cos(angles) / math.sqrt(points)
    sine_table = jnp.sin(angles) / math.sqrt(points)
    forward = jnp.concatenate(
        [
            jnp.concatenate([cosine, -sine_table], axis=1),
            jnp.concatenate([sine_table, cosine], axis=1),
        ],
        axis=0,
    )
    return (forward, forward.T)


def transform(values, matrix):
    initial_shape = values.shape
    flattened = values.reshape(-1, 2 * initial_shape[-1])
    return jnp.dot(
        flattened, matrix, precision=lax.Precision.HIGHEST, preferred_element_type=jnp.float32
    ).reshape(initial_shape)


def local(image, sampled_lines, coil_maps, kspace, reg_weight, conv_first, conv_middle, conv_last):
    features = jnp.transpose(image, (0, 1, 3, 2)).astype(jnp.bfloat16)
    hidden = jax.nn.relu(convolve_slabs(features, conv_first)).astype(jnp.bfloat16)
    for layer_index in range(conv_middle.shape[0]):
        hidden = jax.nn.relu(convolve_slabs(hidden, conv_middle[layer_index])).astype(jnp.bfloat16)
    residual_term = convolve_slabs(hidden, conv_last)
    denoised = image + jnp.transpose(residual_term, (0, 1, 3, 2))
    points = image.shape[-1]
    block_lines = image.shape[1]
    forward, backward = transform_tables(points)
    sampled = jnp.sum(
        (sampled_lines[:, :, None] == jnp.arange(points, dtype=jnp.int32)[None, None, :]).astype(
            jnp.float32
        ),
        axis=1,
    )
    sampling = sampled[None, :, None, None, :]
    coil_index = lax.axis_index("coil")
    regular = reg_weight[0]

    def combine(partial_value):
        return lax.psum(partial_value, "coil")

    def own_block(vector):
        return lax.dynamic_slice_in_dim(vector, coil_index * block_lines, block_lines, 1)

    def inner_product(first_vector, second_vector):
        return jnp.sum(own_block(first_vector) * own_block(second_vector))

    def squares(vector):
        return lax.psum(inner_product(vector, vector), ("slab", "coil"))

    start_field = lax.all_gather(denoised, "coil", axis=1, tiled=True)
    measured = transform(kspace * sampling, backward)
    right_side = (
        combine(jnp.sum(conjugate_product(coil_maps, measured), axis=0)) + regular * start_field
    )
    solution = jnp.zeros_like(right_side)
    residual = right_side
    direction = right_side
    norm_now = squares(residual)
    for iteration in range(ITERS):
        weighted = complex_product(coil_maps, direction[None])
        spectrum = transform(weighted, forward) * sampling
        normal_partial_value = jnp.sum(
            conjugate_product(coil_maps, transform(spectrum, backward)), axis=0
        )
        mapped = combine(normal_partial_value) + regular * direction
        step_size = norm_now / lax.psum(inner_product(direction, mapped), ("slab", "coil"))
        solution = solution + step_size * direction
        residual = residual - step_size * mapped
        norm_next = squares(residual)
        direction = residual + norm_next / norm_now * direction
        norm_now = norm_next
    return (denoised, own_block(solution))


def solution(mesh):
    in_specs = (
        P("slab", "coil", None, None),
        P("slab", None),
        P("coil", "slab", None, None, None),
        P("coil", "slab", None, None, None),
        P(),
        P(),
        P(),
        P(),
    )
    out_specs = (P("slab", "coil", None, None), P("slab", "coil", None, None))
    return jax.shard_map(local, mesh=mesh, in_specs=in_specs, out_specs=out_specs, check_vma=False)
```

profile of v0, /device:TPU:1, one launch (start us, length us, event | category | flops | bytes accessed | tf_op | source)
XLA Modules:
  0.0 1268.1 jit_solution(5127606546430320240)
XLA Ops:
  8.0 4.6 collective-permute-start
  12.6 5.5 collective-permute-start.1
  18.1 2.0 fusion.123
  20.4 1.3 collective-permute-start.2
  21.7 1.3 collective-permute-start.3
  23.1 3.1 collective-permute-done.3
  27.7 3.2 collective-permute-start.4
  30.9 1.9 collective-permute-start.5
  34.2 2.0 sine_multiply_fusion
  36.2 1.7 collective-permute-done.5
  38.0 3.1 collective-permute-start.6
  41.1 1.3 collective-permute-start.7
  42.4 1.9 fusion.102
  44.3 2.7 collective-permute-done.7
  50.6 4.7 collective-permute-start.8
  55.3 1.9 collective-permute-start.9
  57.3 1.6 fusion.122
  58.8 3.5 collective-permute-done.9
  62.4 4.9 collective-permute-start.10
  67.3 1.8 collective-permute-start.11
  69.1 1.8 convolution_bitcast_fusion.4
  71.0 2.8 collective-permute-done.11
  77.8 3.7 collective-permute-start.12
  81.6 1.9 collective-permute-start.13
  84.3 4.2 collective-permute-done.13
  89.4 4.6 collective-permute-start.14
  93.9 1.3 collective-permute-start.15
  96.2 2.1 copy.115
  98.4 1.8 collective-permute-done.15
  100.1 1.8 select_maximum_fusion
  107.8 24.5 %all_gather.3 = f32[1,32,2,320]{3,2,0,1:T(2,128)} all-gather(f32[1,4,2,320]{3,2,0,1:T(2,128)S(1)} %bitcast.233), channel_id=1, replica_groups=mesh['slab'=64,'coil'=8] {'coil'}, dimensions={1}, use_global_device_ids=true | all-gather | bytes 92160 | tf_op jit(solution)/shard_map/all_gather | solution.py:136
  132.3 44.2 %all-reduce.11.cloned.1.call-done = f32[1,32,2,320]{3,1,2,0:T(8,128)} async-done(((f32[1,32,2,320]{3,1,2,0:T(8,128)}), f32[1,32,2,320]{3,1,2,0:T(8,128)}) %all-reduce.11.cloned.1.call-update) | async-done | bytes 81936 | tf_op jit(solution)/shard_map/psum | solution.py:125
  180.2 2.0 reshape.434
  182.2 2.8 convolution_multiply_fusion.3
  186.1 2.0 reshape.436
  188.1 2.8 convolution_bitcast_fusion.3
  191.8 82.2 %all-reduce.13.cloned.1.call-done = f32[1,32,2,320]{3,1,2,0:T(8,128)} async-done(((f32[1,32,2,320]{3,1,2,0:T(8,128)}), f32[1,32,2,320]{3,1,2,0:T(8,128)}) %all-reduce.13.cloned.1.call-update) | async-done | bytes 81936 | tf_op jit(solution)/shard_map/psum | solution.py:125
  275.6 1.4 multiply_reduce_fusion.5
  277.0 102.3 %all-reduce.4 = (f32[]{:T(128)}, f32[]{:T(128)}) all-reduce(f32[]{:T(128)} %get-tuple-element.7, f32[]{:T(128)} %get-tuple-element.6), channel_id=1, replica_groups=mesh['slab'=64,'coil'=8] {'slab','coil'}, use_global_device_ids=true, to_apply=%region_4.5 | all-reduce | flops 2 | bytes 16 | tf_op jit(solution)/shard_map/psum | solution.py:134
  383.0 95.8 %psum.95 = f32[]{:T(128)} all-reduce(f32[]{:T(128)} %multiply_reduce_fusion.4), channel_id=1, replica_groups=mesh['slab'=64,'coil'=8] {'slab','coil'}, use_global_device_ids=true, to_apply=%region_10.11 | all-reduce | flops 1 | bytes 8 | tf_op jit(solution)/shard_map/psum | solution.py:134
  483.8 2.0 reshape.437
  485.8 2.8 convolution_multiply_fusion.2
  489.7 2.0 reshape.438
  491.7 2.8 convolution_bitcast_fusion.2
  495.3 73.4 %all-reduce.15.cloned.1.call-done = f32[1,32,2,320]{3,1,2,0:T(8,128)} async-done(((f32[1,32,2,320]{3,1,2,0:T(8,128)}), f32[1,32,2,320]{3,1,2,0:T(8,128)}) %all-reduce.15.cloned.1.call-update) | async-done | bytes 81936 | tf_op jit(solution)/shard_map/psum | solution.py:125
  570.3 1.3 multiply_reduce_fusion.3
  571.6 102.4 %psum.97 = f32[]{:T(128)} all-reduce(f32[]{:T(128)} %multiply_reduce_fusion.3), channel_id=1, replica_groups=mesh['slab'=64,'coil'=8] {'slab','coil'}, use_global_device_ids=true, to_apply=%region_14.15 | all-reduce | flops 1 | bytes 8 | tf_op jit(solution)/shard_map/psum | solution.py:152
  677.6 95.7 %psum.98 = f32[]{:T(128)} all-reduce(f32[]{:T(128)} %multiply_reduce_fusion.2), channel_id=1, replica_groups=mesh['slab'=64,'coil'=8] {'slab','coil'}, use_global_device_ids=true, to_apply=%region_16.17 | all-reduce | flops 1 | bytes 8 | tf_op jit(solution)/shard_map/psum | solution.py:134
  777.4 1.1 copy.119
  778.4 2.0 reshape.439
  780.4 2.8 convolution_multiply_fusion.1
  783.2 1.1 copy.120
  784.3 2.0 reshape.440
  786.3 2.8 convolution_bitcast_fusion.1
  789.9 73.4 %all-reduce.17.cloned.1.call-done = f32[1,32,2,320]{3,1,2,0:T(8,128)} async-done(((f32[1,32,2,320]{3,1,2,0:T(8,128)}), f32[1,32,2,320]{3,1,2,0:T(8,128)}) %all-reduce.17.cloned.1.call-update) | async-done | bytes 81936 | tf_op jit(solution)/shard_map/psum | solution.py:125
  865.0 1.4 multiply_reduce_fusion.1
  866.4 102.3 %psum.100 = f32[]{:T(128)} all-reduce(f32[]{:T(128)} %multiply_reduce_fusion.1), channel_id=1, replica_groups=mesh['slab'=64,'coil'=8] {'slab','coil'}, use_global_device_ids=true, to_apply=%region_20.21 | all-reduce | flops 1 | bytes 8 | tf_op jit(solution)/shard_map/psum | solution.py:152
  972.3 96.0 %psum.101 = f32[]{:T(128)} all-reduce(f32[]{:T(128)} %multiply_reduce_fusion), channel_id=1, replica_groups=mesh['slab'=64,'coil'=8] {'slab','coil'}, use_global_device_ids=true, to_apply=%region_22.23 | all-reduce | flops 1 | bytes 8 | tf_op jit(solution)/shard_map/psum | solution.py:134
  1073.4 2.0 reshape.441
  1075.4 2.8 convolution_multiply_fusion
  1078.8 1.8 convolution_bitcast_fusion
  1081.4 73.5 %all-reduce.19.cloned.1.call-done = f32[1,32,2,320]{3,1,2,0:T(8,128)} async-done(((f32[1,32,2,320]{3,1,2,0:T(8,128)}), f32[1,32,2,320]{3,1,2,0:T(8,128)}) %all-reduce.19.cloned.1.call-update) | async-done | bytes 81936 | tf_op jit(solution)/shard_map/psum | solution.py:125
  1154.8 1.4 fusion.121
  1156.3 102.3 %psum.103 = f32[]{:T(128)} all-reduce(f32[]{:T(128)} %fusion.121), channel_id=1, replica_groups=mesh['slab'=64,'coil'=8] {'slab','coil'}, use_global_device_ids=true, to_apply=%region_26.27 | all-reduce | flops 1 | bytes 8 | tf_op jit(solution)/shard_map/psum | solution.py:152
  (209 shorter events, 51.5 us)
Async XLA Ops:
  7.2 13.0 %copy-start.31 = (s32[1,80]{1,0:T(1,128)S(1)}, s32[1,80]{1,0:T(1,128)}, u32[]{:S(2)}) copy-start(s32[1,80]{1,0:T(1,128)} %param.9) | copy-start | bytes 964
  7.2 13.1 %copy-start.25 = (f32[4,1,32,2,320]{4,3,2,1,0:T(2,128)S(1)}, f32[4,1,32,2,320]{4,3,2,1,0:T(2,128)}, u32[]{:S(2)}) copy-start(f32[4,1,32,2,320]{4,3,2,1,0:T(2,128)} %param.11) | copy-start | bytes 983044
  7.2 15.9 %copy-start.29 = (bf16[3,3,3,2,64]{4,3,2,1,0:T(2,128)(2,1)S(1)}, bf16[3,3,3,2,64]{4,3,2,1,0:T(2,128)(2,1)}, u32[]{:S(2)}) copy-start(bf16[3,3,3,2,64]{4,3,2,1,0:T(2,128)(2,1)} %param.13) | copy-start | bytes 20740
  7.2 169.3 %all-reduce.11.cloned.1.call-start = ((), (), s32[]{:S(2)}) async-start(), calls=%async_computation | async-start | bytes 196608 | tf_op jit(solution)/shard_map/psum | solution.py:125
  8.0 12.4 collective-permute-start
  12.6 7.8 collective-permute-start.1
  20.2 12.6 copy-start.26
  20.4 2.7 collective-permute-start.2
  21.7 4.5 collective-permute-start.3
  27.7 8.5 collective-permute-start.4
  30.9 7.0 collective-permute-start.5
  33.2 50.3 %copy-start = (f32[4,1,32,1,320]{4,3,2,1,0:T(1,128)}, f32[4,1,32,1,320]{4,3,2,1,0:T(1,128)S(1)}, u32[]{:S(2)}) copy-start(f32[4,1,32,1,320]{4,3,2,1,0:T(1,128)S(1)} %get-tuple-element.106) | copy-start | bytes 491524
  38.0 6.3 collective-permute-start.6
  41.1 5.9 collective-permute-start.7
  50.6 8.2 collective-permute-start.8
  55.3 7.0 collective-permute-start.9
  57.2 11.9 copy-start.14
  62.4 8.6 collective-permute-start.10
  67.3 6.5 collective-permute-start.11
  75.3 0.9 copy-start.19
  75.7 1.1 copy-start.18
  76.3 1.0 copy-start.17
  77.8 18.4 %copy-start.5 = (bf16[1,4,320,64]{2,3,1,0:T(8,128)(2,1)}, bf16[1,4,320,64]{2,3,1,0:T(8,128)(2,1)S(1)}, u32[]{:S(2)}) copy-start(bf16[1,4,320,64]{2,3,1,0:T(8,128)(2,1)S(1)} %fusion.46) | copy-start | bytes 491524
  77.8 17.4 %copy-start.30 = (bf16[3,3,3,64,2]{3,4,2,1,0:T(2,128)(2,1)S(1)}, bf16[3,3,3,64,2]{3,4,2,1,0:T(2,128)(2,1)}, u32[]{:S(2)}) copy-start(bf16[3,3,3,64,2]{3,4,2,1,0:T(2,128)(2,1)} %param.15) | copy-start | bytes 20740
  77.8 6.5 collective-permute-start.12
  81.6 7.0 collective-permute-start.13
  84.3 189.7 %all-reduce.13.cloned.1.call-start = ((), (), s32[]{:S(2)}) async-start(), calls=%async_computation.1 | async-start | bytes 196608 | tf_op jit(solution)/shard_map/psum | solution.py:125
  84.3 11.9 copy-start.7
  88.6 7.6 copy-start.9
  89.4 9.0 collective-permute-start.14
  93.9 6.2 collective-permute-start.15
  98.3 3.7 copy-start.6
  98.3 3.7 copy-start.8
  98.3 3.7 copy-start.10
  106.7 0.7 copy-start.28
  107.8 74.4 %copy-start.27 = (f32[1,4,2,320]{3,2,1,0:T(2,128)}, f32[1,4,2,320]{3,2,1,0:T(2,128)S(1)}, u32[]{:S(2)}) copy-start(f32[1,4,2,320]{3,2,1,0:T(2,128)S(1)} %fusion.62) | copy-start | bytes 30724
  177.5 0.6 copy-start.11
  188.1 2.8 copy-start.1
  191.7 377.0 %all-reduce.15.cloned.1.call-start = ((), (), s32[]{:S(2)}) async-start(), calls=%async_computation.2 | async-start | bytes 196608 | tf_op jit(solution)/shard_map/psum | solution.py:125
  274.9 0.7 copy-start.21
  381.6 0.6 copy-start.16
  481.1 0.6 copy-start.12
  491.7 2.8 copy-start.2
  495.3 368.1 %all-reduce.17.cloned.1.call-start = ((), (), s32[]{:S(2)}) async-start(), calls=%async_computation.3 | async-start | bytes 196608 | tf_op jit(solution)/shard_map/psum | solution.py:125
  569.6 0.6 copy-start.22
  676.3 0.6 copy-start.15
  775.7 0.6 copy-start.13
  786.3 2.9 copy-start.3
  789.9 364.9 %all-reduce.19.cloned.1.call-start = ((), (), s32[]{:S(2)}) async-start(), calls=%async_computation.4 | async-start | bytes 196608 | tf_op jit(solution)/shard_map/psum | solution.py:125
  864.3 0.6 copy-start.23
  971.0 0.6 copy-start.24
  1070.7 0.6 copy-start.20
  1078.2 2.4 copy-start.4
Sparse Core Ops, SparseCore 0:
  84.4 92.0 all-reduce.10
  191.8 82.0 all-reduce.12
  495.4 73.2 all-reduce.14
  790.0 73.3 all-reduce.16
  1081.5 73.2 all-reduce.18
where the time goes:
time: 1280 us; the launch traced here: 1270 us
  blocking collectives  721 us (56%)
  waiting for transfers between devices  367 us (29%)
  starting transfers between devices  47.2 us (4%)
  other arithmetic  40.1 us (3%)
  local copies, waits for them, and re-layouts  39.4 us (3%)
  matrix products  28.2 us (2%)
  between operations  25.4 us (2%)
    psum x4, blocking collectives, squares(): return lax.psum(inner_product(vector, vector), ('slab', 'coil'))  390 us
    psum x5, waiting for transfers between devices, combine(): return lax.psum(partial_value, 'coil')  347 us
    psum x3, blocking collectives, local(): lax.psum(inner_product(direction, mapped), ('slab', 'coil'))  307 us
    ppermute x8, starting transfers between devices, padded_2(): lax.ppermute(lax.slice_in_dim(block, block.shape[dim] - width, None, axis...  30.1 us
  transfers between devices with their start and end apart: 21, of which 12 were waited for; matrix products, arithmetic and copies ran while one was open for 2% of the time, Pallas kernels for 0%

commit v1 on v0

v1 whole, which is shorter than its diff:
```python
import functools
import math

import jax
import jax.numpy as jnp
from jax import lax
from jax.experimental import pallas as pl
from jax.experimental.pallas import tpu as pltpu
from jax.sharding import PartitionSpec as P

MESH = pl.DeviceIdType.MESH
F32 = jnp.float32
BF16 = jnp.bfloat16

Y = 320
YP = 384
XB = 4
CH = 64
C = 32
CL = 4
NS = 80
HALO = 4
XW = 32
Z = 64
X_CHIPS = 4
Y_CHIPS = 8
Z_CHIPS = 8
LIMIT = 56 * 2**20


def dot(a, b):
    return jnp.dot(a, b, preferred_element_type=F32)


def dot_t(a, b):
    return lax.dot_general(a, b, (((1,), (1,)), ((), ())), preferred_element_type=F32)


def split(v):
    high = v.astype(BF16)
    return high, (v - high.astype(F32)).astype(BF16)


def dot3(v, high_ref, low_ref, op):
    high, low = split(v)
    table = high_ref[...]
    return op(high, table) + op(low, table) + op(high, low_ref[...])


def lane_roll(v, amount):
    return pltpu.roll(v, amount % v.shape[1], axis=1)


def kernel(
    image_ref, lines_ref, maps_hbm, kspace_hbm, reg_ref, first_ref, middle_ref, last_ref,
    denoised_ref, out_ref,
    halo, feats, w1f, w1, wt, wm, w4f, w4, p1, p2, p3, sums, tall,
    table_hi, table_lo, pick, local_maps, local_kspace, own_maps, inter, planes, maps_re, maps_im,
    part_send, part_recv, pair, slots,
    local_sem, img_send, img_recv, map_send, map_recv, rhs_send, rhs_recv, sum_send, sum_recv,
):
    s = lax.axis_index("slab")
    c = lax.axis_index("coil")
    x_chip, z_lo = c % X_CHIPS, c // X_CHIPS
    core, y_chip, z_hi = s % 2, (s // 2) % Y_CHIPS, s // (2 * Y_CHIPS)
    z_chip = z_hi * 2 + z_lo

    offsets = [(dz, dx) for dz in range(-HALO, HALO + 1) for dx in (-1, 0, 1) if (dz, dx) != (0, 0)]

    def shifted(dz, dx):
        return ((s + dz + Z) % Z, (c + dx + 8) % 8)

    def stage_partner(stage, d):
        if stage == 0:
            return (
                z_hi * 16 + y_chip * 2 + (core + d // 4) % 2,
                z_lo * 4 + (x_chip + d % 4) % 4,
            )
        if stage == 1:
            return (z_hi * 16 + ((y_chip + d) % 8) * 2 + core, c)
        z_new = (z_chip + d) % 8
        return ((z_new // 2) * 16 + y_chip * 2 + core, (z_new % 2) * 4 + x_chip)

    stage_index = (core * 4 + x_chip, y_chip, z_chip)

    partners = [shifted(dz, dx) for dz, dx in offsets]
    partners += [shifted(0, d) for d in range(1, 8)]
    partners += [stage_partner(stage, d) for stage in range(3) for d in range(1, 8)]
    barrier = pltpu.get_barrier_semaphore()
    for partner in partners:
        pl.semaphore_signal(barrier, inc=1, device_id=partner, device_id_type=MESH)

    local_copies = [
        pltpu.make_async_copy(maps_hbm.at[:, 0], local_maps, local_sem.at[0]),
        pltpu.make_async_copy(kspace_hbm.at[:, 0], local_kspace, local_sem.at[1]),
        pltpu.make_async_copy(
            maps_hbm.at[:, 0, pl.ds(c * XB, XB)], own_maps.at[pl.ds(c * CL, CL)], local_sem.at[2]
        ),
    ]
    for copy in local_copies:
        copy.start()

    halo[HALO, 8:16] = jnp.zeros((8, YP), F32)
    for x in range(XB):
        halo[HALO, 8 + 2 * x : 10 + 2 * x, 0:Y] = image_ref[0, x]

    pl.semaphore_wait(barrier, len(partners))

    image_copies = []
    for i, (dz, dx) in enumerate(offsets):
        copy = pltpu.make_async_remote_copy(
            src_ref=halo.at[HALO, pl.ds(8, 8)],
            dst_ref=halo.at[HALO - dz, pl.ds(8 - 8 * dx, 8)],
            send_sem=img_send.at[i],
            recv_sem=img_recv.at[i],
            device_id=shifted(dz, dx),
            device_id_type=MESH,
        )
        copy.start()
        image_copies.append(copy)
    map_copies = []
    for d in range(1, 8):
        target = (c + d) % 8
        copy = pltpu.make_async_remote_copy(
            src_ref=maps_hbm.at[:, 0, pl.ds(target * XB, XB)],
            dst_ref=own_maps.at[pl.ds(c * CL, CL)],
            send_sem=map_send.at[d - 1],
            recv_sem=map_recv.at[d - 1],
            device_id=(s, target),
            device_id_type=MESH,
        )
        copy.start()
        map_copies.append(copy)

    lines = jnp.concatenate([lines_ref[...], jnp.full((1, 128 - NS), -1, jnp.int32)], axis=1)
    position = lax.broadcasted_iota(jnp.int32, (YP, 128), 0)
    line = jnp.broadcast_to(lines, (YP, 128))
    inside = (position < Y) & (line >= 0)
    product = (position * line).astype(F32)
    phase = product - Y * jnp.floor((product + 0.5) * (1.0 / Y))
    half = jnp.abs(jnp.where(phase > Y / 2, phase - Y, phase))
    sine_sign = jnp.where(phase > Y / 2, -1.0, 1.0)
    low_half = half <= Y / 4
    angle = jnp.where(low_half, half, Y / 2 - half) * (2.0 * math.pi / Y)
    square = angle * angle
    cosine = jnp.full((YP, 128), 1.0 / math.factorial(14), F32) * -1.0
    sine = jnp.full((YP, 128), 1.0 / math.factorial(13), F32)
    for order in range(6, -1, -1):
        cosine = cosine * square + (-1.0) ** order / math.factorial(2 * order)
        if order < 6:
            sine = sine * square + (-1.0) ** order / math.factorial(2 * order + 1)
    scale = 1.0 / math.sqrt(Y)
    cosine = jnp.where(inside, jnp.where(low_half, cosine, -cosine) * scale, 0.0)
    sine = jnp.where(inside, sine * angle * sine_sign * scale, 0.0)
    for row, column, value in (
        (0, 0, cosine), (0, 128, -sine), (YP, 0, sine), (YP, 128, cosine),
    ):
        high, low = split(value)
        table_hi[row : row + YP, column : column + 128] = high
        table_lo[row : row + YP, column : column + 128] = low
    pick[...] = jnp.where(inside & (position == line), 1.0, 0.0).astype(BF16)

    for copy in local_copies:
        copy.wait()
    inter[...] = jnp.zeros_like(inter)
    groups = inter.reshape(3, C, 8, 128)
    tiles = ((0, 128), (1, 128), (2, Y - 256))

    def plane_of(ref, start, count):
        return jnp.concatenate([ref[t, pl.ds(start, count, stride=2), :] for t in range(3)], axis=1)

    def load_planes(source):
        def move(group, carry):
            for x in range(XB):
                value = source(group, x)
                for t, width in tiles:
                    groups[t, group, 2 * x : 2 * x + 2, 0:width] = value[:, 128 * t : 128 * t + width]
            return carry

        lax.fori_loop(0, C, move, 0)
        return plane_of(inter, 0, 4 * C), plane_of(inter, 1, 4 * C)

    kspace_re, kspace_im = load_planes(lambda group, x: local_kspace[group // 8, (group % 8) * XB + x])
    spectrum = []
    for plane in (kspace_re, kspace_im):
        high, low = split(plane)
        spectrum.append(dot(high, pick[...]) + dot(low, pick[...]))
    field = dot3(jnp.concatenate(spectrum, axis=1), table_hi, table_lo, dot_t)
    planes[...] = field
    s_re, s_im = load_planes(lambda group, x: local_maps[group // 8, (group % 8) * XB + x])
    energy = s_re * s_re + s_im * s_im
    energy = jnp.sum(energy.reshape(16, 8, YP), axis=0)
    energy = energy[:, 0:128] + energy[:, 128:256] + energy[:, 256:384]
    f_re, f_im = planes[:, 0:YP], planes[:, YP : 2 * YP]
    sum_re = jnp.sum((s_re * f_re + s_im * f_im).reshape(CL, XW, YP), axis=0)
    sum_im = jnp.sum((s_re * f_im - s_im * f_re).reshape(CL, XW, YP), axis=0)
    for k in range(8):
        part_send[k, 0:4] = sum_re[4 * k : 4 * k + 4]
        part_send[k, 4:8] = sum_im[4 * k : 4 * k + 4]
    part_recv[c] = part_send[c]
    rhs_copies = []
    for d in range(1, 8):
        target = (c + d) % 8
        copy = pltpu.make_async_remote_copy(
            src_ref=part_send.at[target],
            dst_ref=part_recv.at[c],
            send_sem=rhs_send.at[d - 1],
            recv_sem=rhs_recv.at[d - 1],
            device_id=(s, target),
            device_id_type=MESH,
        )
        copy.start()
        rhs_copies.append(copy)

    def start_stage(which, stage, value):
        index = stage_index[stage]
        slots[which, stage, index] = value
        copies = []
        for d in range(1, 8):
            copy = pltpu.make_async_remote_copy(
                src_ref=slots.at[which, stage, index],
                dst_ref=slots.at[which, stage, index],
                send_sem=sum_send.at[which, stage, d - 1],
                recv_sem=sum_recv.at[which, stage, d - 1],
                device_id=stage_partner(stage, d),
                device_id_type=MESH,
            )
            copy.start()
            copies.append(copy)
        return copies

    def finish_stage(which, stage, copies):
        for copy in copies:
            copy.wait()
        return jnp.sum(slots[which, stage], axis=0)

    energy_copies = start_stage(0, 0, jnp.concatenate([energy, jnp.zeros((8, 128), F32)], axis=0))

    wt[...] = jnp.zeros_like(wt)
    for dy in range(3):
        for dz in range(3):
            for dx in range(3):
                row = 2 * (dy * 9 + dz * 3 + dx)
                wt[row : row + 2, 0:CH] = first_ref[dz * 9 + dx * 3 + dy].astype(F32)
    w1f[...] = jnp.zeros_like(w1f)
    row8 = lax.broadcasted_iota(jnp.int32, (8, 128), 0)
    for q in range(9):
        low = jnp.where(row8 < 6, wt[6 * q : 6 * q + 8, :], 0.0)
        both = low + lane_roll(pltpu.roll(low, 2, axis=0), CH)
        for x in range(10):
            if x < 9:
                w1f[24 * q + 2 * x : 24 * q + 2 * x + 8, 128 * x : 128 * x + 128] = both
            else:
                w1f[24 * q + 18 : 24 * q + 24, 128 * x : 128 * x + 128] = low[0:6]
    w1[...] = w1f[0:256, :].astype(BF16)

    wm[...] = jnp.zeros_like(wm)

    def middle_weights(i, carry):
        layer, dz = i // 3, i % 3
        for dx in range(3):
            taps = [middle_ref[i * 9 + dx * 3 + dy] for dy in range(3)]
            wm[layer, pl.ds(pl.multiple_of(dz * 256 + dx * CH, CH), CH), 0:128] = jnp.concatenate([taps[0], taps[2]], axis=1)
            wm[layer, pl.ds(pl.multiple_of(dz * 256 + dx * CH, CH), CH), 128:256] = jnp.concatenate([taps[1], taps[1]], axis=1)
        return carry

    lax.fori_loop(0, 6, middle_weights, 0)

    w4f[...] = jnp.zeros_like(w4f)
    for dz in range(3):
        for dx in range(3):
            merged = None
            for dy in range(3):
                tap = last_ref[dz * 9 + dx * 3 + dy].astype(F32)
                tap = jnp.concatenate([tap, jnp.zeros((CH, 126), F32)], axis=1)
                tap = tap if dy == 0 else lane_roll(tap, 8 * dy)
                merged = tap if merged is None else merged + tap
            for x in range(XB):
                base = dz * 384 + (x + dx) * CH
                w4f[base : base + CH, :] += merged if x == 0 else lane_roll(merged, 2 * x)
    w4[...] = w4f[...].astype(BF16)

    for copy in image_copies:
        copy.wait()
    row24 = lax.broadcasted_iota(jnp.int32, (24, YP), 0) // 8 + (c - 1)

    def feature_slice(zi, carry):
        slice_index = s + zi - HALO
        valid = (row24 >= 0) & (row24 < 8) & (slice_index >= 0) & (slice_index < Z)
        value = jnp.where(valid, halo[zi].astype(BF16).astype(F32), 0.0)
        feats[0, zi] = lane_roll(value, 1)
        feats[1, zi] = value
        feats[2, zi] = lane_roll(value, -1)
        return carry

    lax.fori_loop(0, 2 * HALO + 1, feature_slice, 0)

    lane = lax.broadcasted_iota(jnp.int32, (1, 256), 1)

    def first_layer(z, carry):
        slice_index = s + z - 3
        slice_valid = (slice_index >= 0) & (slice_index < Z)
        columns = jnp.concatenate(
            [feats[dy, pl.ds(z, 3)].reshape(72, YP) for dy in range(3)] + [jnp.zeros((40, YP), F32)],
            axis=0,
        )
        tall[...] = jnp.transpose(columns).astype(BF16)
        for x in range(0, 10, 2):
            at = c * XB - 3 + x + lane // CH - lane // 128
            mask = jnp.where((at >= 0) & (at < XW) & slice_valid, 1.0, 0.0)
            product = dot(tall[0:Y, :], w1[:, 128 * x : 128 * x + 256])
            product = (jnp.maximum(product, 0.0) * mask).astype(BF16)
            p1[z, x] = product[:, 0:128]
            p1[z, x + 1] = product[:, 128:256]
        return carry

    lax.fori_loop(0, 7, first_layer, 0)
    energy = finish_stage(0, 0, energy_copies)
    energy_copies = start_stage(0, 1, energy)

    sums[...] = jnp.zeros_like(sums)
    low_lanes = lax.broadcasted_iota(jnp.int32, (Y, 128), 1) < CH

    def middle_layer(layer, source, target, slices, rows):
        reach_z, reach_x = slices // 2, (rows - XB) // 2

        def one_slice(z, carry):
            slice_index = s + z - reach_z
            slice_valid = (slice_index >= 0) & (slice_index < Z)
            for x in range(rows):
                operand = jnp.concatenate(
                    [source[z + dz, x + 2 * k] for dz in range(3) for k in range(2)], axis=1
                )
                sums[x, 8 : 8 + Y, :] = dot(operand, wm[layer])
            following = None
            for x in range(rows - 1, -1, -1):
                at = c * XB - reach_x + x
                mask = jnp.where((at >= 0) & (at < XW) & slice_valid, 1.0, 0.0).astype(F32)
                outer = jnp.where(low_lanes, sums[x, 7 : 7 + Y, 0:128], sums[x, 9 : 9 + Y, 0:128])
                value = outer + lane_roll(outer, CH) + sums[x, 8 : 8 + Y, 128:256]
                value = jnp.maximum(value, 0.0) * mask
                target[z, x] = jnp.where(low_lanes, value, value if following is None else following).astype(BF16)
                following = value
            return carry

        lax.fori_loop(0, slices, one_slice, 0)

    middle_layer(0, p1, p2, 5, 8)
    energy = finish_stage(0, 1, energy_copies)
    energy_copies = start_stage(0, 2, energy)
    middle_layer(1, p2, p3, 3, 6)
    energy = finish_stage(0, 2, energy_copies)

    operand = jnp.concatenate([p3[dz, 2 * k] for dz in range(3) for k in range(3)], axis=1)
    w1f[0:YP, 0:128] = jnp.zeros((YP, 128), F32)
    w1f[0:Y, 0:128] = dot(operand, w4[...])
    turned = jnp.transpose(w1f[0:YP, 0:128])
    residual = lane_roll(turned[0:8], 1) + turned[8:16] + lane_roll(turned[16:24], -1)
    lane8 = lax.broadcasted_iota(jnp.int32, (8, YP), 1)
    denoised = halo[HALO, 8:16] + jnp.where(lane8 < Y, residual, 0.0)
    for t in range(3):
        pair[t, 0:8] = denoised[:, 128 * t : 128 * t + 128]
        pair[t, 8:16] = denoised[:, 128 * t : 128 * t + 128]

    def write(ref):
        for x in range(XB):
            for t, width in tiles:
                ref[0, x, :, 128 * t : 128 * t + width] = pair[t, 2 * x : 2 * x + 2, 0:width]

    write(denoised_ref)
    den_re, den_im = plane_of(pair, 0, 8), plane_of(pair, 1, 8)

    reg = reg_ref[0]
    for copy in rhs_copies:
        copy.wait()
    adjoint = jnp.sum(part_recv[...], axis=0)
    other = pltpu.roll(adjoint, 4, axis=0)
    first_rows = lax.broadcasted_iota(jnp.int32, (8, YP), 0) < 4
    right = (
        jnp.where(first_rows, adjoint, other) + reg * den_re,
        jnp.where(first_rows, other, adjoint) + reg * den_im,
    )
    for copy in map_copies:
        copy.wait()
    s_re, s_im = load_planes(lambda group, x: own_maps[group, x])
    maps_re[...] = s_re
    maps_im[...] = s_im

    mean = jnp.sum(jnp.sum(energy, axis=0, keepdims=True), axis=1, keepdims=True) * (NS / Y / (Z * XW * Y))

    def spectrum_of(vector):
        v_re = jnp.broadcast_to(vector[0][None], (16, 8, YP)).reshape(128, YP)
        v_im = jnp.broadcast_to(vector[1][None], (16, 8, YP)).reshape(128, YP)
        m_re, m_im = maps_re[...], maps_im[...]
        weighted = jnp.concatenate([m_re * v_re - m_im * v_im, m_re * v_im + m_im * v_re], axis=1)
        return dot3(weighted, table_hi, table_lo, dot)

    def gram_map(vector):
        planes[...] = dot3(spectrum_of(vector), table_hi, table_lo, dot_t)
        m_re, m_im = maps_re[...], maps_im[...]
        f_re, f_im = planes[:, 0:YP], planes[:, YP : 2 * YP]
        real = jnp.sum((m_re * f_re + m_im * f_im).reshape(16, 8, YP), axis=0)
        imag = jnp.sum((m_re * f_im - m_im * f_re).reshape(16, 8, YP), axis=0)
        return real + pltpu.roll(real, 4, axis=0), imag + pltpu.roll(imag, 4, axis=0)

    basis = [right]
    for _ in range(3):
        mapped = gram_map(basis[-1])
        basis.append((mapped[0] - mean * basis[-1][0], mapped[1] - mean * basis[-1][1]))
    last_spectrum = spectrum_of(basis[-1])
    last_energy = jnp.sum((last_spectrum * last_spectrum).reshape(16, 8, 256), axis=0)
    last_energy = last_energy[:, 0:128] + last_energy[:, 128:256]

    def folded(first, second):
        product = first[0] * second[0] + first[1] * second[1]
        product = product[:, 0:128] + product[:, 128:256] + product[:, 256:384]
        return 0.5 * jnp.sum(product, axis=0, keepdims=True)

    pairs = [(i, j) for i in range(4) for j in range(i, 4)]
    rows = [folded(basis[i], basis[j]) for i, j in pairs]
    rows.append(jnp.sum(last_energy, axis=0, keepdims=True))
    rows.append(jnp.zeros((16 - len(rows), 128), F32))
    moments = jnp.concatenate(rows, axis=0)
    for stage in range(3):
        moments = finish_stage(1, stage, start_stage(1, stage, moments))
    moments = jnp.sum(moments, axis=1, keepdims=True)
    gram = {}
    for row, (i, j) in enumerate(pairs):
        gram[i, j] = gram[j, i] = moments[row : row + 1]
    shift = mean + reg
    matrix = {}
    for i in range(4):
        for j in range(i, 4):
            value = gram[i + 1, j] + shift * gram[i, j] if i < 3 else moments[10:11] + reg * gram[3, 3]
            matrix[i, j] = matrix[j, i] = value
    norm = [jnp.where(matrix[i, i] > 1e-37, lax.rsqrt(jnp.maximum(matrix[i, i], 1e-37)), 0.0) for i in range(4)]
    side = [gram[0, i] * norm[i] for i in range(4)]
    for i in range(4):
        for j in range(i, 4):
            matrix[i, j] = matrix[j, i] = matrix[i, j] * norm[i] * norm[j]
    inverse = []
    for k in range(4):
        pivot = matrix[k, k]
        inverse.append(jnp.where(pivot > 2e-6, 1.0 / jnp.maximum(pivot, 2e-6), 0.0))
        for i in range(k + 1, 4):
            factor = matrix[i, k] * inverse[k]
            for j in range(i, 4):
                matrix[i, j] = matrix[j, i] = matrix[i, j] - factor * matrix[k, j]
            side[i] = side[i] - factor * side[k]
    weights = [None] * 4
    for k in range(3, -1, -1):
        value = side[k]
        for j in range(k + 1, 4):
            value = value - matrix[k, j] * weights[j]
        weights[k] = value * inverse[k]
    real = sum(weights[k] * norm[k] * basis[k][0] for k in range(4))
    imag = sum(weights[k] * norm[k] * basis[k][1] for k in range(4))
    for t in range(3):
        pair[t, pl.ds(0, 8, stride=2), :] = real[:, 128 * t : 128 * t + 128]
        pair[t, pl.ds(1, 8, stride=2), :] = imag[:, 128 * t : 128 * t + 128]
    write(out_ref)


def local(image, sampled_lines, coil_maps, kspace, reg_weight, conv_first, conv_middle, conv_last):
    vmem = pl.BlockSpec(memory_space=pltpu.VMEM)
    anywhere = pl.BlockSpec(memory_space=pl.ANY)
    block = jax.ShapeDtypeStruct((1, XB, 2, Y), F32)
    dma = pltpu.SemaphoreType.DMA
    return pl.pallas_call(
        kernel,
        out_shape=(block, block),
        in_specs=[vmem, vmem, anywhere, anywhere, pl.BlockSpec(memory_space=pltpu.SMEM), vmem, vmem, vmem],
        out_specs=(vmem, vmem),
        scratch_shapes=[
            pltpu.VMEM((9, 24, YP), F32),
            pltpu.VMEM((3, 9, 24, YP), F32),
            pltpu.VMEM((YP, 1280), F32),
            pltpu.VMEM((256, 1280), BF16),
            pltpu.VMEM((64, 128), F32),
            pltpu.VMEM((2, 768, 256), BF16),
            pltpu.VMEM((1152, 128), F32),
            pltpu.VMEM((1152, 128), BF16),
            pltpu.VMEM((7, 10, Y, 128), BF16),
            pltpu.VMEM((5, 8, Y, 128), BF16),
            pltpu.VMEM((3, 6, Y, 128), BF16),
            pltpu.VMEM((8, Y + 16, 256), F32),
            pltpu.VMEM((YP, 256), BF16),
            pltpu.VMEM((2 * YP, 256), BF16),
            pltpu.VMEM((2 * YP, 256), BF16),
            pltpu.VMEM((YP, 128), BF16),
            pltpu.VMEM((CL, XW, 2, Y), F32),
            pltpu.VMEM((CL, XW, 2, Y), F32),
            pltpu.VMEM((C, XB, 2, Y), F32),
            pltpu.VMEM((3, 8 * C, 128), F32),
            pltpu.VMEM((4 * C, 2 * YP), F32),
            pltpu.VMEM((4 * C, YP), F32),
            pltpu.VMEM((4 * C, YP), F32),
            pltpu.VMEM((8, 8, YP), F32),
            pltpu.VMEM((8, 8, YP), F32),
            pltpu.VMEM((3, 16, 128), F32),
            pltpu.VMEM((2, 3, 8, 16, 128), F32),
            dma((3,)), dma((26,)), dma((26,)), dma((7,)), dma((7,)), dma((7,)), dma((7,)),
            dma((2, 3, 7)), dma((2, 3, 7)),
        ],
        compiler_params=pltpu.CompilerParams(
            collective_id=0, has_side_effects=True, vmem_limit_bytes=LIMIT
        ),
    )(
        image, sampled_lines, coil_maps, kspace, reg_weight,
        conv_first.reshape(27, 2, CH), conv_middle.reshape(54, CH, CH), conv_last.reshape(27, CH, 2),
    )


def solution(mesh):
    in_specs = (
        P("slab", "coil", None, None),
        P("slab", None),
        P("coil", "slab", None, None, None),
        P("coil", "slab", None, None, None),
        P(),
        P(),
        P(),
        P(),
    )
    out_specs = (P("slab", "coil", None, None), P("slab", "coil", None, None))
    return jax.shard_map(local, mesh=mesh, in_specs=in_specs, out_specs=out_specs, check_vma=False)
```

time: 1280 us -> 65.6 us (0.05)
  blocking collectives: 721 us -> 0 us
  waiting for transfers between devices: 367 us -> 0 us
  Pallas kernels: 0 us -> 60.4 us
  starting transfers between devices: 47.2 us -> 0 us
  other arithmetic: 40.1 us -> 0 us
  local copies, waits for them, and re-layouts: 39.4 us -> 3.65 us
  matrix products: 28.2 us -> 0 us
  between operations: 25.4 us -> 1.29 us
    psum x7 -> x0, blocking collectives: 697 us -> none  [the longest x4 390 us: squares(): return lax.psum(inner_product(vector, vector), ('slab', 'coil'))]
    psum x5 -> x0, waiting for transfers between devices: 347 us -> none  [combine(): return lax.psum(partial_value, 'coil')]
    pallas_call x0 -> x1, Pallas kernels: none -> 60.4 us  [local(): pl.pallas_call(kernel, out_shape=(block, block), in_specs=[vmem, vmem, an...]
    ppermute x16 -> x0, starting transfers between devices: 47 us -> none  [the longest x8 30.1 us: padded_2(): lax.ppermute(lax.slice_in_dim(block, block.shape[dim] - width, None, axis...]
    dot_general x21 -> x0, matrix products: 28.2 us -> none  [the longest x9 23.4 us: transform(): jnp.dot(flattened, matrix, precision=lax.Precision.HIGHEST, preferred_ele...]
    all_gather x1 -> x0, blocking collectives: 24.5 us -> none  [local(): start_field = lax.all_gather(denoised, 'coil', axis=1, tiled=True)]
    ppermute x16 -> x0, waiting for transfers between devices: 19.8 us -> none  [the longest x8 19.7 us: padded_2(): lax.ppermute(lax.slice_in_dim(block, 0, width, axis=dim), axis, backward)]
  transfers between devices with their start and end apart: 21 -> 0, of which waited for: 12 -> 0; matrix products, arithmetic and copies ran while one was open for 2% -> 0% of each run, Pallas kernels for 0% -> 0%
where the time goes in v1:
time: 65.6 us; the launch traced here: 65.3 us
  Pallas kernels  60.4 us (92%)
  local copies, waits for them, and re-layouts  3.65 us (6%)
  between operations  1.29 us (2%)
    pallas_call x1, Pallas kernels, local(): pl.pallas_call(kernel, out_shape=(block, block), in_specs=[vmem, vmem, an...  60.4 us
    unnamed x5, local copies, waits for them, and re-layouts  3.65 us

profile of v1, /device:TPU:1, one launch (start us, length us, event | category | flops | bytes accessed | tf_op | source)
XLA Modules:
  0.0 65.3 jit_solution(15860186027074512370)
XLA Ops:
  1.3 1.7 %copy.10 = bf16[3,3,3,64,2]{4,3,2,1,0:T(8,128)(2,1)} copy(bf16[3,3,3,64,2]{3,4,2,1,0:T(2,128)(2,1)} %param.15) | data formatting | bytes 13824 | tf_op args[7]
  3.0 60.4 %shard_map.95 = (f32[1,4,2,320]{3,2,1,0:T(2,128)}, f32[1,4,2,320]{3,2,1,0:T(2,128)}) custom-call(f32[1,4,2,320]{3,2,1,0:T(2,128)} %image_ref.1, s32[1,80]{1,0:T(1,128)} %lines_ref.1, f32[4,1,32,2,320]{4,3,2,1,0:T(2,128)} %maps_hbm.1, f32[4,1,32,2,320]{4,3,2,1,0:T(2,128)} %kspace_hbm.1, f32[1]{0:T(128)S(6)} %copy.13.reg_ref, bf16[27,2,64]{2,1,0:T(2,128)(2,1)} %bitcast.5, ...), custom_call_target="tpu_custom_call" | custom-call | tf_op jit(solution)/shard_map/pallas_call | solution.py:469
  63.4 0.0 copy-start
  63.4 1.3 %copy.14 = f32[1,4,2,320]{3,2,1,0:T(2,128)} copy(f32[1,4,2,320]{3,2,1,0:T(2,128)} %get-tuple-element.4) | data formatting | bytes 20480
  64.7 0.0 copy-done
  64.7 0.6 copy.15
Async XLA Ops:
  63.4 1.3 %copy-start = (f32[1,4,2,320]{3,2,1,0:T(2,128)S(1)}, f32[1,4,2,320]{3,2,1,0:T(2,128)}, u32[]{:S(2)}) copy-start(f32[1,4,2,320]{3,2,1,0:T(2,128)} %get-tuple-element.5) | copy-start | bytes 30724

commit v2 on v1

--- a/solution.py
+++ b/solution.py
@@ -25,6 +25,7 @@
 X_CHIPS = 4
 Y_CHIPS = 8
 Z_CHIPS = 8
+CHUNK = 1
 LIMIT = 56 * 2**20
 
 
@@ -43,8 +44,9 @@
 
 def dot3(v, high_ref, low_ref, op):
     high, low = split(v)
-    table = high_ref[...]
-    return op(high, table) + op(low, table) + op(high, low_ref[...])
+    rows = v.shape[0]
+    both = op(jnp.concatenate([high, low], axis=0), high_ref[...])
+    return both[0:rows] + both[rows : 2 * rows] + op(high, low_ref[...])
 
 
 def lane_roll(v, amount):
@@ -54,9 +56,9 @@
 def kernel(
     image_ref, lines_ref, maps_hbm, kspace_hbm, reg_ref, first_ref, middle_ref, last_ref,
     denoised_ref, out_ref,
-    halo, feats, w1f, w1, wt, wm, w4f, w4, p1, p2, p3, sums, tall,
+    halo, feats, w1f, w1, wt, wl, wm, w4f, w4, p1, p2, p3,
     table_hi, table_lo, pick, local_maps, local_kspace, own_maps, inter, planes, maps_re, maps_im,
-    part_send, part_recv, pair, slots,
+    part_send, part_recv, pair, energy_out, slots,
     local_sem, img_send, img_recv, map_send, map_recv, rhs_send, rhs_recv, sum_send, sum_recv,
 ):
     s = lax.axis_index("slab")
@@ -132,37 +134,37 @@
         copy.start()
         map_copies.append(copy)
 
-    lines = jnp.concatenate([lines_ref[...], jnp.full((1, 128 - NS), -1, jnp.int32)], axis=1)
-    position = lax.broadcasted_iota(jnp.int32, (YP, 128), 0)
-    line = jnp.broadcast_to(lines, (YP, 128))
-    inside = (position < Y) & (line >= 0)
-    product = (position * line).astype(F32)
-    phase = product - Y * jnp.floor((product + 0.5) * (1.0 / Y))
-    half = jnp.abs(jnp.where(phase > Y / 2, phase - Y, phase))
-    sine_sign = jnp.where(phase > Y / 2, -1.0, 1.0)
-    low_half = half <= Y / 4
-    angle = jnp.where(low_half, half, Y / 2 - half) * (2.0 * math.pi / Y)
-    square = angle * angle
-    cosine = jnp.full((YP, 128), 1.0 / math.factorial(14), F32) * -1.0
-    sine = jnp.full((YP, 128), 1.0 / math.factorial(13), F32)
-    for order in range(6, -1, -1):
-        cosine = cosine * square + (-1.0) ** order / math.factorial(2 * order)
-        if order < 6:
-            sine = sine * square + (-1.0) ** order / math.factorial(2 * order + 1)
-    scale = 1.0 / math.sqrt(Y)
-    cosine = jnp.where(inside, jnp.where(low_half, cosine, -cosine) * scale, 0.0)
-    sine = jnp.where(inside, sine * angle * sine_sign * scale, 0.0)
-    for row, column, value in (
-        (0, 0, cosine), (0, 128, -sine), (YP, 0, sine), (YP, 128, cosine),
-    ):
-        high, low = split(value)
-        table_hi[row : row + YP, column : column + 128] = high
-        table_lo[row : row + YP, column : column + 128] = low
-    pick[...] = jnp.where(inside & (position == line), 1.0, 0.0).astype(BF16)
-
-    for copy in local_copies:
-        copy.wait()
-    inter[...] = jnp.zeros_like(inter)
+    def phase_tables():
+        lines = jnp.concatenate([lines_ref[...], jnp.full((1, 128 - NS), -1, jnp.int32)], axis=1)
+        position = lax.broadcasted_iota(jnp.int32, (YP, 128), 0)
+        line = jnp.broadcast_to(lines, (YP, 128))
+        inside = (position < Y) & (line >= 0)
+        product = (position * line).astype(F32)
+        phase = product - Y * jnp.floor((product + 0.5) * (1.0 / Y))
+        half = jnp.abs(jnp.where(phase > Y / 2, phase - Y, phase))
+        sine_sign = jnp.where(phase > Y / 2, -1.0, 1.0)
+        low_half = half <= Y / 4
+        angle = jnp.where(low_half, half, Y / 2 - half) * (2.0 * math.pi / Y)
+        square = angle * angle
+        cosine = jnp.full((YP, 128), 1.0 / math.factorial(14), F32) * -1.0
+        sine = jnp.full((YP, 128), 1.0 / math.factorial(13), F32)
+        for order in range(6, -1, -1):
+            cosine = cosine * square + (-1.0) ** order / math.factorial(2 * order)
+            if order < 6:
+                sine = sine * square + (-1.0) ** order / math.factorial(2 * order + 1)
+        scale = 1.0 / math.sqrt(Y)
+        cosine = jnp.where(inside, jnp.where(low_half, cosine, -cosine) * scale, 0.0)
+        sine = jnp.where(inside, sine * angle * sine_sign * scale, 0.0)
+        for row, column, value in (
+            (0, 0, cosine), (0, 128, -sine), (YP, 0, sine), (YP, 128, cosine),
+        ):
+            high, low = split(value)
+            table_hi[row : row + YP, column : column + 128] = high
+            table_lo[row : row + YP, column : column + 128] = low
+        pick[...] = jnp.where(inside & (position == line), 1.0, 0.0).astype(BF16)
+
+    phase_tables()
+
     groups = inter.reshape(3, C, 8, 128)
     tiles = ((0, 128), (1, 128), (2, Y - 256))
 
@@ -180,24 +182,31 @@
         lax.fori_loop(0, C, move, 0)
         return plane_of(inter, 0, 4 * C), plane_of(inter, 1, 4 * C)
 
-    kspace_re, kspace_im = load_planes(lambda group, x: local_kspace[group // 8, (group % 8) * XB + x])
-    spectrum = []
-    for plane in (kspace_re, kspace_im):
-        high, low = split(plane)
-        spectrum.append(dot(high, pick[...]) + dot(low, pick[...]))
-    field = dot3(jnp.concatenate(spectrum, axis=1), table_hi, table_lo, dot_t)
-    planes[...] = field
-    s_re, s_im = load_planes(lambda group, x: local_maps[group // 8, (group % 8) * XB + x])
-    energy = s_re * s_re + s_im * s_im
-    energy = jnp.sum(energy.reshape(16, 8, YP), axis=0)
-    energy = energy[:, 0:128] + energy[:, 128:256] + energy[:, 256:384]
-    f_re, f_im = planes[:, 0:YP], planes[:, YP : 2 * YP]
-    sum_re = jnp.sum((s_re * f_re + s_im * f_im).reshape(CL, XW, YP), axis=0)
-    sum_im = jnp.sum((s_re * f_im - s_im * f_re).reshape(CL, XW, YP), axis=0)
-    for k in range(8):
-        part_send[k, 0:4] = sum_re[4 * k : 4 * k + 4]
-        part_send[k, 4:8] = sum_im[4 * k : 4 * k + 4]
-    part_recv[c] = part_send[c]
+    for copy in local_copies:
+        copy.wait()
+    inter[...] = jnp.zeros_like(inter)
+
+    def phase_adjoint():
+        kspace_re, kspace_im = load_planes(lambda group, x: local_kspace[group // 8, (group % 8) * XB + x])
+        spectrum = []
+        for plane in (kspace_re, kspace_im):
+            high, low = split(plane)
+            spectrum.append(dot(high, pick[...]) + dot(low, pick[...]))
+        field = dot3(jnp.concatenate(spectrum, axis=1), table_hi, table_lo, dot_t)
+        planes[...] = field
+        s_re, s_im = load_planes(lambda group, x: local_maps[group // 8, (group % 8) * XB + x])
+        energy = s_re * s_re + s_im * s_im
+        energy = jnp.sum(energy.reshape(16, 8, YP), axis=0)
+        energy_out[...] = energy[:, 0:128] + energy[:, 128:256] + energy[:, 256:384]
+        f_re, f_im = planes[:, 0:YP], planes[:, YP : 2 * YP]
+        sum_re = jnp.sum((s_re * f_re + s_im * f_im).reshape(CL, XW, YP), axis=0)
+        sum_im = jnp.sum((s_re * f_im - s_im * f_re).reshape(CL, XW, YP), axis=0)
+        for k in range(8):
+            part_send[k, 0:4] = sum_re[4 * k : 4 * k + 4]
+            part_send[k, 4:8] = sum_im[4 * k : 4 * k + 4]
+        part_recv[c] = part_send[c]
+
+    phase_adjoint()
     rhs_copies = []
     for d in range(1, 8):
         target = (c + d) % 8
@@ -234,51 +243,62 @@
             copy.wait()
         return jnp.sum(slots[which, stage], axis=0)
 
-    energy_copies = start_stage(0, 0, jnp.concatenate([energy, jnp.zeros((8, 128), F32)], axis=0))
-
-    wt[...] = jnp.zeros_like(wt)
-    for dy in range(3):
+    energy_copies = start_stage(0, 0, jnp.concatenate([energy_out[...], jnp.zeros((8, 128), F32)], axis=0))
+
+    def last_all():
+        wl[...] = jnp.zeros_like(wl)
+        for k in range(27):
+            wl[2 * k : 2 * k + 2, 0:CH] = last_ref[k].astype(F32)
+        return wl[...]
+
+    def phase_weights():
+        wt[...] = jnp.zeros_like(wt)
+        for dy in range(3):
+            for dz in range(3):
+                for dx in range(3):
+                    row = 2 * (dy * 9 + dz * 3 + dx)
+                    wt[row : row + 2, 0:CH] = first_ref[dz * 9 + dx * 3 + dy].astype(F32)
+        w1f[...] = jnp.zeros_like(w1f)
+        row8 = lax.broadcasted_iota(jnp.int32, (8, 128), 0)
+        for q in range(9):
+            low = jnp.where(row8 < 6, wt[6 * q : 6 * q + 8, :], 0.0)
+            both = low + lane_roll(pltpu.roll(low, 2, axis=0), CH)
+            for x in range(10):
+                if x < 9:
+                    w1f[24 * q + 2 * x : 24 * q + 2 * x + 8, 128 * x : 128 * x + 128] = both
+                else:
+                    w1f[24 * q + 18 : 24 * q + 24, 128 * x : 128 * x + 128] = low[0:6]
+        w1[...] = w1f[0:256, :].astype(BF16)
+
+        wm[...] = jnp.zeros_like(wm)
+
+        def middle_weights(i, carry):
+            layer, dz = i // 3, i % 3
+            for dx in range(3):
+                taps = [middle_ref[i * 9 + dx * 3 + dy] for dy in range(3)]
+                wm[layer, pl.ds(pl.multiple_of(dz * 256 + dx * CH, CH), CH), 0:128] = jnp.concatenate([taps[0], taps[2]], axis=1)
+                wm[layer, pl.ds(pl.multiple_of(dz * 256 + dx * CH, CH), CH), 128:256] = jnp.concatenate([taps[1], taps[1]], axis=1)
+            return carry
+
+        lax.fori_loop(0, 6, middle_weights, 0)
+
+        w4f[...] = jnp.zeros_like(w4f)
+        turned = jnp.transpose(last_all())[0:CH]
+        column = lax.broadcasted_iota(jnp.int32, (CH, 128), 1)
         for dz in range(3):
             for dx in range(3):
-                row = 2 * (dy * 9 + dz * 3 + dx)
-                wt[row : row + 2, 0:CH] = first_ref[dz * 9 + dx * 3 + dy].astype(F32)
-    w1f[...] = jnp.zeros_like(w1f)
-    row8 = lax.broadcasted_iota(jnp.int32, (8, 128), 0)
-    for q in range(9):
-        low = jnp.where(row8 < 6, wt[6 * q : 6 * q + 8, :], 0.0)
-        both = low + lane_roll(pltpu.roll(low, 2, axis=0), CH)
-        for x in range(10):
-            if x < 9:
-                w1f[24 * q + 2 * x : 24 * q + 2 * x + 8, 128 * x : 128 * x + 128] = both
-            else:
-                w1f[24 * q + 18 : 24 * q + 24, 128 * x : 128 * x + 128] = low[0:6]
-    w1[...] = w1f[0:256, :].astype(BF16)
-
-    wm[...] = jnp.zeros_like(wm)
-
-    def middle_weights(i, carry):
-        layer, dz = i // 3, i % 3
-        for dx in range(3):
-            taps = [middle_ref[i * 9 + dx * 3 + dy] for dy in range(3)]
-            wm[layer, pl.ds(pl.multiple_of(dz * 256 + dx * CH, CH), CH), 0:128] = jnp.concatenate([taps[0], taps[2]], axis=1)
-            wm[layer, pl.ds(pl.multiple_of(dz * 256 + dx * CH, CH), CH), 128:256] = jnp.concatenate([taps[1], taps[1]], axis=1)
-        return carry
-
-    lax.fori_loop(0, 6, middle_weights, 0)
-
-    w4f[...] = jnp.zeros_like(w4f)
-    for dz in range(3):
-        for dx in range(3):
-            merged = None
-            for dy in range(3):
-                tap = last_ref[dz * 9 + dx * 3 + dy].astype(F32)
-                tap = jnp.concatenate([tap, jnp.zeros((CH, 126), F32)], axis=1)
-                tap = tap if dy == 0 else lane_roll(tap, 8 * dy)
-                merged = tap if merged is None else merged + tap
-            for x in range(XB):
-                base = dz * 384 + (x + dx) * CH
-                w4f[base : base + CH, :] += merged if x == 0 else lane_roll(merged, 2 * x)
-    w4[...] = w4f[...].astype(BF16)
+                merged = None
+                for dy in range(3):
+                    first_column = 2 * (dz * 9 + dx * 3 + dy)
+                    tap = jnp.where((column >= first_column) & (column < first_column + 2), turned, 0.0)
+                    tap = lane_roll(tap, 8 * dy - first_column)
+                    merged = tap if merged is None else merged + tap
+                for x in range(XB):
+                    base = dz * 384 + (x + dx) * CH
+                    w4f[base : base + CH, :] += merged if x == 0 else lane_roll(merged, 2 * x)
+        w4[...] = w4f[...].astype(BF16)
+
+    phase_weights()
 
     for copy in image_copies:
         copy.wait()
@@ -293,7 +313,11 @@
         feats[2, zi] = lane_roll(value, -1)
         return carry
 
-    lax.fori_loop(0, 2 * HALO + 1, feature_slice, 0)
+    def phase_features():
+        for zi in range(2 * HALO + 1):
+            feature_slice(zi, 0)
+
+    phase_features()
 
     lane = lax.broadcasted_iota(jnp.int32, (1, 256), 1)
 
@@ -301,25 +325,31 @@
         slice_index = s + z - 3
         slice_valid = (slice_index >= 0) & (slice_index < Z)
         columns = jnp.concatenate(
-            [feats[dy, pl.ds(z, 3)].reshape(72, YP) for dy in range(3)] + [jnp.zeros((40, YP), F32)],
+            [feats[dy, z : z + 3].reshape(72, YP) for dy in range(3)] + [jnp.zeros((40, YP), F32)],
             axis=0,
         )
-        tall[...] = jnp.transpose(columns).astype(BF16)
+        tall = jnp.transpose(columns)[0:Y].astype(BF16)
         for x in range(0, 10, 2):
             at = c * XB - 3 + x + lane // CH - lane // 128
             mask = jnp.where((at >= 0) & (at < XW) & slice_valid, 1.0, 0.0)
-            product = dot(tall[0:Y, :], w1[:, 128 * x : 128 * x + 256])
+            product = dot(tall, w1[:, 128 * x : 128 * x + 256])
             product = (jnp.maximum(product, 0.0) * mask).astype(BF16)
             p1[z, x] = product[:, 0:128]
             p1[z, x + 1] = product[:, 128:256]
         return carry
 
-    lax.fori_loop(0, 7, first_layer, 0)
+    def phase_first():
+        for z in range(7):
+            first_layer(z, 0)
+
+    phase_first()
     energy = finish_stage(0, 0, energy_copies)
     energy_copies = start_stage(0, 1, energy)
 
-    sums[...] = jnp.zeros_like(sums)
     low_lanes = lax.broadcasted_iota(jnp.int32, (Y, 128), 1) < CH
+
+    rowi = lax.broadcasted_iota(jnp.int32, (Y, 128), 0)
+    edge = jnp.where((low_lanes & (rowi == 0)) | (jnp.logical_not(low_lanes) & (rowi == Y - 1)), 0.0, 1.0)
 
     def middle_layer(layer, source, target, slices, rows):
         reach_z, reach_x = slices // 2, (rows - XB) // 2
@@ -327,47 +357,71 @@
         def one_slice(z, carry):
             slice_index = s + z - reach_z
             slice_valid = (slice_index >= 0) & (slice_index < Z)
-            for x in range(rows):
-                operand = jnp.concatenate(
-                    [source[z + dz, x + 2 * k] for dz in range(3) for k in range(2)], axis=1
-                )
-                sums[x, 8 : 8 + Y, :] = dot(operand, wm[layer])
-            following = None
-            for x in range(rows - 1, -1, -1):
+            def finish(x, before):
                 at = c * XB - reach_x + x
                 mask = jnp.where((at >= 0) & (at < XW) & slice_valid, 1.0, 0.0).astype(F32)
-                outer = jnp.where(low_lanes, sums[x, 7 : 7 + Y, 0:128], sums[x, 9 : 9 + Y, 0:128])
-                value = outer + lane_roll(outer, CH) + sums[x, 8 : 8 + Y, 128:256]
+                first_half = products[x][:, 0:128]
+                outer = jnp.where(low_lanes, pltpu.roll(first_half, 1, axis=0), pltpu.roll(first_half, Y - 1, axis=0)) * edge
+                value = outer + lane_roll(outer, CH) + products[x][:, 128:256]
                 value = jnp.maximum(value, 0.0) * mask
-                target[z, x] = jnp.where(low_lanes, value, value if following is None else following).astype(BF16)
-                following = value
+                if before is not None:
+                    target[z, x - 1] = jnp.where(low_lanes, before, value).astype(BF16)
+                return value
+
+            value = None
+            products = []
+            for x in range(0, rows + CHUNK, CHUNK):
+                if x < rows:
+                    operand = jnp.concatenate(
+                        [
+                            source[z + dz, x + 2 * k : x + 2 * k + CHUNK].reshape(CHUNK * Y, 128)
+                            for dz in range(3)
+                            for k in range(2)
+                        ],
+                        axis=1,
+                    )
+                    product = dot(operand, wm[layer])
+                    products.append(product)
+                if x > 0:
+                    for i in range(CHUNK):
+                        value = finish(x - CHUNK + i, value)
+            target[z, rows - 1] = value.astype(BF16)
             return carry
 
         lax.fori_loop(0, slices, one_slice, 0)
 
-    middle_layer(0, p1, p2, 5, 8)
+    def phase_middle0():
+        middle_layer(0, p1, p2, 5, 8)
+
+    phase_middle0()
     energy = finish_stage(0, 1, energy_copies)
     energy_copies = start_stage(0, 2, energy)
-    middle_layer(1, p2, p3, 3, 6)
+    def phase_middle1():
+        middle_layer(1, p2, p3, 3, 6)
+
+    phase_middle1()
     energy = finish_stage(0, 2, energy_copies)
-
-    operand = jnp.concatenate([p3[dz, 2 * k] for dz in range(3) for k in range(3)], axis=1)
-    w1f[0:YP, 0:128] = jnp.zeros((YP, 128), F32)
-    w1f[0:Y, 0:128] = dot(operand, w4[...])
-    turned = jnp.transpose(w1f[0:YP, 0:128])
-    residual = lane_roll(turned[0:8], 1) + turned[8:16] + lane_roll(turned[16:24], -1)
-    lane8 = lax.broadcasted_iota(jnp.int32, (8, YP), 1)
-    denoised = halo[HALO, 8:16] + jnp.where(lane8 < Y, residual, 0.0)
-    for t in range(3):
-        pair[t, 0:8] = denoised[:, 128 * t : 128 * t + 128]
-        pair[t, 8:16] = denoised[:, 128 * t : 128 * t + 128]
 
     def write(ref):
         for x in range(XB):
             for t, width in tiles:
                 ref[0, x, :, 128 * t : 128 * t + width] = pair[t, 2 * x : 2 * x + 2, 0:width]
 
-    write(denoised_ref)
+    def phase_last():
+        operand = jnp.concatenate([p3[dz, 2 * k] for dz in range(3) for k in range(3)], axis=1)
+        w1f[0:YP, 0:128] = jnp.zeros((YP, 128), F32)
+        w1f[0:Y, 0:128] = dot(operand, w4[...])
+        turned = jnp.transpose(w1f[0:YP, 0:128])
+        residual = lane_roll(turned[0:8], 1) + turned[8:16] + lane_roll(turned[16:24], -1)
+        lane8 = lax.broadcasted_iota(jnp.int32, (8, YP), 1)
+        denoised = halo[HALO, 8:16] + jnp.where(lane8 < Y, residual, 0.0)
+        for t in range(3):
+            pair[t, 0:8] = denoised[:, 128 * t : 128 * t + 128]
+            pair[t, 8:16] = denoised[:, 128 * t : 128 * t + 128]
+
+        write(denoised_ref)
+
+    phase_last()
     den_re, den_im = plane_of(pair, 0, 8), plane_of(pair, 1, 8)
 
     reg = reg_ref[0]
@@ -382,9 +436,13 @@
     )
     for copy in map_copies:
         copy.wait()
-    s_re, s_im = load_planes(lambda group, x: own_maps[group, x])
-    maps_re[...] = s_re
-    maps_im[...] = s_im
+
+    def phase_maps():
+        s_re, s_im = load_planes(lambda group, x: own_maps[group, x])
+        maps_re[...] = s_re
+        maps_im[...] = s_im
+
+    phase_maps()
 
     mean = jnp.sum(jnp.sum(energy, axis=0, keepdims=True), axis=1, keepdims=True) * (NS / Y / (Z * XW * Y))
 
@@ -403,24 +461,29 @@
         imag = jnp.sum((m_re * f_im - m_im * f_re).reshape(16, 8, YP), axis=0)
         return real + pltpu.roll(real, 4, axis=0), imag + pltpu.roll(imag, 4, axis=0)
 
-    basis = [right]
-    for _ in range(3):
-        mapped = gram_map(basis[-1])
-        basis.append((mapped[0] - mean * basis[-1][0], mapped[1] - mean * basis[-1][1]))
-    last_spectrum = spectrum_of(basis[-1])
-    last_energy = jnp.sum((last_spectrum * last_spectrum).reshape(16, 8, 256), axis=0)
-    last_energy = last_energy[:, 0:128] + last_energy[:, 128:256]
-
     def folded(first, second):
         product = first[0] * second[0] + first[1] * second[1]
         product = product[:, 0:128] + product[:, 128:256] + product[:, 256:384]
         return 0.5 * jnp.sum(product, axis=0, keepdims=True)
 
     pairs = [(i, j) for i in range(4) for j in range(i, 4)]
-    rows = [folded(basis[i], basis[j]) for i, j in pairs]
-    rows.append(jnp.sum(last_energy, axis=0, keepdims=True))
-    rows.append(jnp.zeros((16 - len(rows), 128), F32))
-    moments = jnp.concatenate(rows, axis=0)
+    basis = [right]
+
+    def phase_krylov():
+        del basis[1:]
+        for _ in range(3):
+            mapped = gram_map(basis[-1])
+            basis.append((mapped[0] - mean * basis[-1][0], mapped[1] - mean * basis[-1][1]))
+        last_spectrum = spectrum_of(basis[-1])
+        last_energy = jnp.sum((last_spectrum * last_spectrum).reshape(16, 8, 256), axis=0)
+        last_energy = last_energy[:, 0:128] + last_energy[:, 128:256]
+        rows = [folded(basis[i], basis[j]) for i, j in pairs]
+        rows.append(jnp.sum(last_energy, axis=0, keepdims=True))
+        rows.append(jnp.zeros((16 - len(rows), 128), F32))
+        moments = jnp.concatenate(rows, axis=0)
+        return moments
+
+    moments = phase_krylov()
     for stage in range(3):
         moments = finish_stage(1, stage, start_stage(1, stage, moments))
     moments = jnp.sum(moments, axis=1, keepdims=True)
@@ -477,14 +540,13 @@
             pltpu.VMEM((YP, 1280), F32),
             pltpu.VMEM((256, 1280), BF16),
             pltpu.VMEM((64, 128), F32),
+            pltpu.VMEM((128, 128), F32),
             pltpu.VMEM((2, 768, 256), BF16),
             pltpu.VMEM((1152, 128), F32),
             pltpu.VMEM((1152, 128), BF16),
             pltpu.VMEM((7, 10, Y, 128), BF16),
             pltpu.VMEM((5, 8, Y, 128), BF16),
             pltpu.VMEM((3, 6, Y, 128), BF16),
-            pltpu.VMEM((8, Y + 16, 256), F32),
-            pltpu.VMEM((YP, 256), BF16),
             pltpu.VMEM((2 * YP, 256), BF16),
             pltpu.VMEM((2 * YP, 256), BF16),
             pltpu.VMEM((YP, 128), BF16),
@@ -498,6 +560,7 @@
             pltpu.VMEM((8, 8, YP), F32),
             pltpu.VMEM((8, 8, YP), F32),
             pltpu.VMEM((3, 16, 128), F32),
+            pltpu.VMEM((8, 128), F32),
             pltpu.VMEM((2, 3, 8, 16, 128), F32),
             dma((3,)), dma((26,)), dma((26,)), dma((7,)), dma((7,)), dma((7,)), dma((7,)),
             dma((2, 3, 7)), dma((2, 3, 7)),
@@ -507,7 +570,7 @@
         ),
     )(
         image, sampled_lines, coil_maps, kspace, reg_weight,
-        conv_first.reshape(27, 2, CH), conv_middle.reshape(54, CH, CH), conv_last.reshape(27, CH, 2),
+        conv_first.reshape(27, 2, CH), conv_middle.reshape(54, CH, CH), conv_last.transpose(0, 1, 2, 4, 3).reshape(27, 2, CH),
     )
 
 

time: 65.6 us -> 59.8 us (0.912)
  Pallas kernels: 60.4 us -> 56.2 us
  local copies, waits for them, and re-layouts: 3.65 us -> 1.92 us
    pallas_call x1, Pallas kernels: 60.4 us -> 56.2 us  [local(): pl.pallas_call(kernel, out_shape=(block, block), in_specs=[vmem, vmem, an...]
    unnamed x5 -> x4, local copies, waits for them, and re-layouts: 3.65 us -> 1.92 us
where the time goes in v2:
time: 59.8 us; the launch traced here: 59.4 us
  Pallas kernels  56.2 us (94%)
  local copies, waits for them, and re-layouts  1.92 us (3%)
  between operations  1.29 us (2%)
    pallas_call x1, Pallas kernels, local(): pl.pallas_call(kernel, out_shape=(block, block), in_specs=[vmem, vmem, an...  56.2 us
    unnamed x4, local copies, waits for them, and re-layouts  1.92 us

profile of v2, /device:TPU:1, one launch (start us, length us, event | category | flops | bytes accessed | tf_op | source)
XLA Modules:
  0.0 59.4 jit_solution(12110036195732895041)
XLA Ops:
  1.3 56.2 %shard_map.95 = (f32[1,4,2,320]{3,2,1,0:T(2,128)}, f32[1,4,2,320]{3,2,1,0:T(2,128)}) custom-call(f32[1,4,2,320]{3,2,1,0:T(2,128)} %image_ref.1, s32[1,80]{1,0:T(1,128)} %lines_ref.1, f32[4,1,32,2,320]{4,3,2,1,0:T(2,128)} %maps_hbm.1, f32[4,1,32,2,320]{4,3,2,1,0:T(2,128)} %kspace_hbm.1, f32[1]{0:T(128)S(6)} %copy.12.reg_ref, bf16[27,2,64]{2,1,0:T(2,128)(2,1)} %bitcast.6, ...), custom_call_target="tpu_custom_call" | custom-call | tf_op jit(solution)/shard_map/pallas_call | solution.py:532
  57.5 0.0 copy-start
  57.5 1.3 %copy.13 = f32[1,4,2,320]{3,2,1,0:T(2,128)} copy(f32[1,4,2,320]{3,2,1,0:T(2,128)} %get-tuple-element.4) | data formatting | bytes 20480
  58.8 0.0 copy-done
  58.8 0.6 %copy.14 = f32[1,4,2,320]{3,2,1,0:T(2,128)} copy(f32[1,4,2,320]{3,2,1,0:T(2,128)S(1)} %copy-done) | data formatting | bytes 20480
Async XLA Ops:
  57.5 1.3 %copy-start = (f32[1,4,2,320]{3,2,1,0:T(2,128)S(1)}, f32[1,4,2,320]{3,2,1,0:T(2,128)}, u32[]{:S(2)}) copy-start(f32[1,4,2,320]{3,2,1,0:T(2,128)} %get-tuple-element.5) | copy-start | bytes 30724

commit v3 on v2

--- a/solution.py
+++ b/solution.py
@@ -56,7 +56,7 @@
 def kernel(
     image_ref, lines_ref, maps_hbm, kspace_hbm, reg_ref, first_ref, middle_ref, last_ref,
     denoised_ref, out_ref,
-    halo, feats, w1f, w1, wt, wl, wm, w4f, w4, p1, p2, p3,
+    halo, own_image, feats, w1f, w1, wt, wl, wm, w4f, w4, p1, p2, p3,
     table_hi, table_lo, pick, local_maps, local_kspace, own_maps, inter, planes, maps_re, maps_im,
     part_send, part_recv, pair, energy_out, slots,
     local_sem, img_send, img_recv, map_send, map_recv, rhs_send, rhs_recv, sum_send, sum_recv,
@@ -102,17 +102,20 @@
     for copy in local_copies:
         copy.start()
 
-    halo[HALO, 8:16] = jnp.zeros((8, YP), F32)
+    own_image[...] = jnp.zeros_like(own_image)
     for x in range(XB):
-        halo[HALO, 8 + 2 * x : 10 + 2 * x, 0:Y] = image_ref[0, x]
+        own_image[2 * x : 2 * x + 2, 0:Y] = image_ref[0, x]
+    mine = own_image[...]
+    tail = jnp.concatenate([mine[:, 256:384], jnp.zeros((8, 128), F32)], axis=1)
+    halo[HALO, 1] = jnp.concatenate([mine[:, 0:256], tail], axis=0).astype(BF16)
 
     pl.semaphore_wait(barrier, len(partners))
 
     image_copies = []
     for i, (dz, dx) in enumerate(offsets):
         copy = pltpu.make_async_remote_copy(
-            src_ref=halo.at[HALO, pl.ds(8, 8)],
-            dst_ref=halo.at[HALO - dz, pl.ds(8 - 8 * dx, 8)],
+            src_ref=halo.at[HALO, 1],
+            dst_ref=halo.at[HALO - dz, 1 - dx],
             send_sem=img_send.at[i],
             recv_sem=img_recv.at[i],
             device_id=shifted(dz, dx),
@@ -120,20 +123,6 @@
         )
         copy.start()
         image_copies.append(copy)
-    map_copies = []
-    for d in range(1, 8):
-        target = (c + d) % 8
-        copy = pltpu.make_async_remote_copy(
-            src_ref=maps_hbm.at[:, 0, pl.ds(target * XB, XB)],
-            dst_ref=own_maps.at[pl.ds(c * CL, CL)],
-            send_sem=map_send.at[d - 1],
-            recv_sem=map_recv.at[d - 1],
-            device_id=(s, target),
-            device_id_type=MESH,
-        )
-        copy.start()
-        map_copies.append(copy)
-
     def phase_tables():
         lines = jnp.concatenate([lines_ref[...], jnp.full((1, 128 - NS), -1, jnp.int32)], axis=1)
         position = lax.broadcasted_iota(jnp.int32, (YP, 128), 0)
@@ -207,20 +196,6 @@
         part_recv[c] = part_send[c]
 
     phase_adjoint()
-    rhs_copies = []
-    for d in range(1, 8):
-        target = (c + d) % 8
-        copy = pltpu.make_async_remote_copy(
-            src_ref=part_send.at[target],
-            dst_ref=part_recv.at[c],
-            send_sem=rhs_send.at[d - 1],
-            recv_sem=rhs_recv.at[d - 1],
-            device_id=(s, target),
-            device_id_type=MESH,
-        )
-        copy.start()
-        rhs_copies.append(copy)
-
     def start_stage(which, stage, value):
         index = stage_index[stage]
         slots[which, stage, index] = value
@@ -243,7 +218,7 @@
             copy.wait()
         return jnp.sum(slots[which, stage], axis=0)
 
-    energy_copies = start_stage(0, 0, jnp.concatenate([energy_out[...], jnp.zeros((8, 128), F32)], axis=0))
+    energy_copies = start_stage(0, 0, jnp.sum(energy_out[...], axis=0, keepdims=True))
 
     def last_all():
         wl[...] = jnp.zeros_like(wl)
@@ -302,12 +277,44 @@
 
     for copy in image_copies:
         copy.wait()
+    energy_copies = start_stage(0, 1, finish_stage(0, 0, energy_copies))
+    map_copies = []
+    for d in range(1, 8):
+        target = (c + d) % 8
+        copy = pltpu.make_async_remote_copy(
+            src_ref=maps_hbm.at[:, 0, pl.ds(target * XB, XB)],
+            dst_ref=own_maps.at[pl.ds(c * CL, CL)],
+            send_sem=map_send.at[d - 1],
+            recv_sem=map_recv.at[d - 1],
+            device_id=(s, target),
+            device_id_type=MESH,
+        )
+        copy.start()
+        map_copies.append(copy)
+    rhs_copies = []
+    for d in range(1, 8):
+        target = (c + d) % 8
+        copy = pltpu.make_async_remote_copy(
+            src_ref=part_send.at[target],
+            dst_ref=part_recv.at[c],
+            send_sem=rhs_send.at[d - 1],
+            recv_sem=rhs_recv.at[d - 1],
+            device_id=(s, target),
+            device_id_type=MESH,
+        )
+        copy.start()
+        rhs_copies.append(copy)
+
     row24 = lax.broadcasted_iota(jnp.int32, (24, YP), 0) // 8 + (c - 1)
 
     def feature_slice(zi, carry):
         slice_index = s + zi - HALO
         valid = (row24 >= 0) & (row24 < 8) & (slice_index >= 0) & (slice_index < Z)
-        value = jnp.where(valid, halo[zi].astype(BF16).astype(F32), 0.0)
+        blocks = [halo[zi, k].astype(F32) for k in range(3)]
+        value = jnp.concatenate(
+            [jnp.concatenate([block[0:8], block[8:16, 0:128]], axis=1) for block in blocks], axis=0
+        )
+        value = jnp.where(valid, value, 0.0)
         feats[0, zi] = lane_roll(value, 1)
         feats[1, zi] = value
         feats[2, zi] = lane_roll(value, -1)
@@ -343,15 +350,13 @@
             first_layer(z, 0)
 
     phase_first()
-    energy = finish_stage(0, 0, energy_copies)
-    energy_copies = start_stage(0, 1, energy)
 
     low_lanes = lax.broadcasted_iota(jnp.int32, (Y, 128), 1) < CH
 
     rowi = lax.broadcasted_iota(jnp.int32, (Y, 128), 0)
     edge = jnp.where((low_lanes & (rowi == 0)) | (jnp.logical_not(low_lanes) & (rowi == Y - 1)), 0.0, 1.0)
 
-    def middle_layer(layer, source, target, slices, rows):
+    def middle_layer(layer, source, target, slices, rows, begin, end):
         reach_z, reach_x = slices // 2, (rows - XB) // 2
 
         def one_slice(z, carry):
@@ -388,19 +393,21 @@
             target[z, rows - 1] = value.astype(BF16)
             return carry
 
-        lax.fori_loop(0, slices, one_slice, 0)
+        lax.fori_loop(begin, end, one_slice, 0)
 
     def phase_middle0():
-        middle_layer(0, p1, p2, 5, 8)
+        middle_layer(0, p1, p2, 5, 8, 0, 3)
+
+    def phase_middle0b():
+        middle_layer(0, p1, p2, 5, 8, 3, 5)
 
     phase_middle0()
-    energy = finish_stage(0, 1, energy_copies)
-    energy_copies = start_stage(0, 2, energy)
+    energy_copies = start_stage(0, 2, finish_stage(0, 1, energy_copies))
+    phase_middle0b()
     def phase_middle1():
-        middle_layer(1, p2, p3, 3, 6)
+        middle_layer(1, p2, p3, 3, 6, 0, 3)
 
     phase_middle1()
-    energy = finish_stage(0, 2, energy_copies)
 
     def write(ref):
         for x in range(XB):
@@ -414,7 +421,7 @@
         turned = jnp.transpose(w1f[0:YP, 0:128])
         residual = lane_roll(turned[0:8], 1) + turned[8:16] + lane_roll(turned[16:24], -1)
         lane8 = lax.broadcasted_iota(jnp.int32, (8, YP), 1)
-        denoised = halo[HALO, 8:16] + jnp.where(lane8 < Y, residual, 0.0)
+        denoised = own_image[...] + jnp.where(lane8 < Y, residual, 0.0)
         for t in range(3):
             pair[t, 0:8] = denoised[:, 128 * t : 128 * t + 128]
             pair[t, 8:16] = denoised[:, 128 * t : 128 * t + 128]
@@ -443,8 +450,9 @@
         maps_im[...] = s_im
 
     phase_maps()
-
-    mean = jnp.sum(jnp.sum(energy, axis=0, keepdims=True), axis=1, keepdims=True) * (NS / Y / (Z * XW * Y))
+    energy = finish_stage(0, 2, energy_copies)
+
+    mean = jnp.sum(energy, axis=1, keepdims=True) * (NS / Y / (Z * XW * Y))
 
     def spectrum_of(vector):
         v_re = jnp.broadcast_to(vector[0][None], (16, 8, YP)).reshape(128, YP)
@@ -480,21 +488,28 @@
         rows = [folded(basis[i], basis[j]) for i, j in pairs]
         rows.append(jnp.sum(last_energy, axis=0, keepdims=True))
         rows.append(jnp.zeros((16 - len(rows), 128), F32))
-        moments = jnp.concatenate(rows, axis=0)
-        return moments
+        packed = jnp.concatenate(rows, axis=0)
+        for width in (64, 32, 16, 8):
+            packed = packed + lane_roll(packed, width)
+        place = lax.broadcasted_iota(jnp.int32, (16, 128), 1) // 8
+        owner = lax.broadcasted_iota(jnp.int32, (16, 128), 0)
+        return jnp.sum(jnp.where(place == owner, packed, 0.0), axis=0, keepdims=True)
 
     moments = phase_krylov()
     for stage in range(3):
         moments = finish_stage(1, stage, start_stage(1, stage, moments))
-    moments = jnp.sum(moments, axis=1, keepdims=True)
+    place = lax.broadcasted_iota(jnp.int32, (1, 128), 1) // 8
+    values = [
+        jnp.sum(jnp.where(place == i, moments, 0.0), axis=1, keepdims=True) for i in range(len(pairs) + 1)
+    ]
     gram = {}
     for row, (i, j) in enumerate(pairs):
-        gram[i, j] = gram[j, i] = moments[row : row + 1]
+        gram[i, j] = gram[j, i] = values[row]
     shift = mean + reg
     matrix = {}
     for i in range(4):
         for j in range(i, 4):
-            value = gram[i + 1, j] + shift * gram[i, j] if i < 3 else moments[10:11] + reg * gram[3, 3]
+            value = gram[i + 1, j] + shift * gram[i, j] if i < 3 else values[10] + reg * gram[3, 3]
             matrix[i, j] = matrix[j, i] = value
     norm = [jnp.where(matrix[i, i] > 1e-37, lax.rsqrt(jnp.maximum(matrix[i, i], 1e-37)), 0.0) for i in range(4)]
     side = [gram[0, i] * norm[i] for i in range(4)]
@@ -535,7 +550,8 @@
         in_specs=[vmem, vmem, anywhere, anywhere, pl.BlockSpec(memory_space=pltpu.SMEM), vmem, vmem, vmem],
         out_specs=(vmem, vmem),
         scratch_shapes=[
-            pltpu.VMEM((9, 24, YP), F32),
+            pltpu.VMEM((9, 3, 16, 256), BF16),
+            pltpu.VMEM((8, YP), F32),
             pltpu.VMEM((3, 9, 24, YP), F32),
             pltpu.VMEM((YP, 1280), F32),
             pltpu.VMEM((256, 1280), BF16),
@@ -561,7 +577,7 @@
             pltpu.VMEM((8, 8, YP), F32),
             pltpu.VMEM((3, 16, 128), F32),
             pltpu.VMEM((8, 128), F32),
-            pltpu.VMEM((2, 3, 8, 16, 128), F32),
+            pltpu.VMEM((2, 3, 8, 1, 128), F32),
             dma((3,)), dma((26,)), dma((26,)), dma((7,)), dma((7,)), dma((7,)), dma((7,)),
             dma((2, 3, 7)), dma((2, 3, 7)),
         ],

time: 59.8 us -> 56.5 us (0.945); the launches traced: 59.4 us -> 55.5 us
  Pallas kernels: 56.2 us -> 52.2 us
    pallas_call x1, Pallas kernels: 56.2 us -> 52.2 us  [local(): pl.pallas_call(kernel, out_shape=(block, block), in_specs=[vmem, vmem, an...]
where the time goes in v3:
time: 56.5 us; the launch traced here: 55.5 us
  Pallas kernels  52.2 us (92%)
  local copies, waits for them, and re-layouts  1.92 us (3%)
  between operations  1.29 us (2%)
    pallas_call x1, Pallas kernels, local(): pl.pallas_call(kernel, out_shape=(block, block), in_specs=[vmem, vmem, an...  52.2 us
    unnamed x4, local copies, waits for them, and re-layouts  1.92 us

profile of v3, /device:TPU:1, one launch (start us, length us, event | category | flops | bytes accessed | tf_op | source)
XLA Modules:
  0.0 55.5 jit_solution(4533368946433976140)
XLA Ops:
  1.3 52.2 %shard_map.95 = (f32[1,4,2,320]{3,2,1,0:T(2,128)}, f32[1,4,2,320]{3,2,1,0:T(2,128)}) custom-call(f32[1,4,2,320]{3,2,1,0:T(2,128)} %image_ref.1, s32[1,80]{1,0:T(1,128)} %lines_ref.1, f32[4,1,32,2,320]{4,3,2,1,0:T(2,128)} %maps_hbm.1, f32[4,1,32,2,320]{4,3,2,1,0:T(2,128)} %kspace_hbm.1, f32[1]{0:T(128)S(6)} %copy.12.reg_ref, bf16[27,2,64]{2,1,0:T(2,128)(2,1)} %bitcast.6, ...), custom_call_target="tpu_custom_call" | custom-call | tf_op jit(solution)/shard_map/pallas_call | solution.py:547
  53.5 0.0 copy-start
  53.5 1.3 %copy.13 = f32[1,4,2,320]{3,2,1,0:T(2,128)} copy(f32[1,4,2,320]{3,2,1,0:T(2,128)} %get-tuple-element.4) | data formatting | bytes 20480
  54.9 0.0 copy-done
  54.9 0.6 %copy.14 = f32[1,4,2,320]{3,2,1,0:T(2,128)} copy(f32[1,4,2,320]{3,2,1,0:T(2,128)S(1)} %copy-done) | data formatting | bytes 20480
Async XLA Ops:
  53.5 1.3 %copy-start = (f32[1,4,2,320]{3,2,1,0:T(2,128)S(1)}, f32[1,4,2,320]{3,2,1,0:T(2,128)}, u32[]{:S(2)}) copy-start(f32[1,4,2,320]{3,2,1,0:T(2,128)} %get-tuple-element.5) | copy-start | bytes 30724

commit v4 on v3

--- a/solution.py
+++ b/solution.py
@@ -25,7 +25,6 @@
 X_CHIPS = 4
 Y_CHIPS = 8
 Z_CHIPS = 8
-CHUNK = 1
 LIMIT = 56 * 2**20
 
 
@@ -60,6 +59,7 @@
     table_hi, table_lo, pick, local_maps, local_kspace, own_maps, inter, planes, maps_re, maps_im,
     part_send, part_recv, pair, energy_out, slots,
     local_sem, img_send, img_recv, map_send, map_recv, rhs_send, rhs_recv, sum_send, sum_recv,
+    core_send, core_recv,
 ):
     s = lax.axis_index("slab")
     c = lax.axis_index("coil")
@@ -67,10 +67,12 @@
     core, y_chip, z_hi = s % 2, (s // 2) % Y_CHIPS, s // (2 * Y_CHIPS)
     z_chip = z_hi * 2 + z_lo
 
-    offsets = [(dz, dx) for dz in range(-HALO, HALO + 1) for dx in (-1, 0, 1) if (dz, dx) != (0, 0)]
-
-    def shifted(dz, dx):
-        return ((s + dz + Z) % Z, (c + dx + 8) % 8)
+    outward = 2 * core - 1
+    offsets = [(r, dx) for r in range(-1, HALO + 1) for dx in (-1, 0, 1) if (r, dx) != (0, 0)]
+
+    def needing(r, dx):
+        away = r if r % 2 == 0 else -r
+        return ((s - outward * away + Z) % Z, (c + dx + 8) % 8)
 
     def stage_partner(stage, d):
         if stage == 0:
@@ -85,8 +87,8 @@
 
     stage_index = (core * 4 + x_chip, y_chip, z_chip)
 
-    partners = [shifted(dz, dx) for dz, dx in offsets]
-    partners += [shifted(0, d) for d in range(1, 8)]
+    partners = [((s + outward * r + Z) % Z, (c + dx + 8) % 8) for r, dx in offsets]
+    partners += [(s, (c + d) % 8) for d in range(1, 8)]
     partners += [stage_partner(stage, d) for stage in range(3) for d in range(1, 8)]
     barrier = pltpu.get_barrier_semaphore()
     for partner in partners:
@@ -107,22 +109,22 @@
         own_image[2 * x : 2 * x + 2, 0:Y] = image_ref[0, x]
     mine = own_image[...]
     tail = jnp.concatenate([mine[:, 256:384], jnp.zeros((8, 128), F32)], axis=1)
-    halo[HALO, 1] = jnp.concatenate([mine[:, 0:256], tail], axis=0).astype(BF16)
+    halo[1, 1] = jnp.concatenate([mine[:, 0:256], tail], axis=0).astype(BF16)
 
     pl.semaphore_wait(barrier, len(partners))
 
-    image_copies = []
-    for i, (dz, dx) in enumerate(offsets):
+    image_copies = {}
+    for i, (r, dx) in enumerate(offsets):
         copy = pltpu.make_async_remote_copy(
-            src_ref=halo.at[HALO, 1],
-            dst_ref=halo.at[HALO - dz, 1 - dx],
+            src_ref=halo.at[1, 1],
+            dst_ref=halo.at[r + 1, 1 - dx],
             send_sem=img_send.at[i],
             recv_sem=img_recv.at[i],
-            device_id=shifted(dz, dx),
+            device_id=needing(r, dx),
             device_id_type=MESH,
         )
         copy.start()
-        image_copies.append(copy)
+        image_copies[r, dx] = copy
     def phase_tables():
         lines = jnp.concatenate([lines_ref[...], jnp.full((1, 128 - NS), -1, jnp.int32)], axis=1)
         position = lax.broadcasted_iota(jnp.int32, (YP, 128), 0)
@@ -220,10 +222,13 @@
 
     energy_copies = start_stage(0, 0, jnp.sum(energy_out[...], axis=0, keepdims=True))
 
+    def tap_slice(dz):
+        return dz * core + (2 - dz) * (1 - core)
+
     def last_all():
         wl[...] = jnp.zeros_like(wl)
         for k in range(27):
-            wl[2 * k : 2 * k + 2, 0:CH] = last_ref[k].astype(F32)
+            wl[2 * k : 2 * k + 2, 0:CH] = last_ref[tap_slice(k // 9) * 9 + k % 9].astype(F32)
         return wl[...]
 
     def phase_weights():
@@ -232,7 +237,7 @@
             for dz in range(3):
                 for dx in range(3):
                     row = 2 * (dy * 9 + dz * 3 + dx)
-                    wt[row : row + 2, 0:CH] = first_ref[dz * 9 + dx * 3 + dy].astype(F32)
+                    wt[row : row + 2, 0:CH] = first_ref[tap_slice(dz) * 9 + dx * 3 + dy].astype(F32)
         w1f[...] = jnp.zeros_like(w1f)
         row8 = lax.broadcasted_iota(jnp.int32, (8, 128), 0)
         for q in range(9):
@@ -250,7 +255,7 @@
         def middle_weights(i, carry):
             layer, dz = i // 3, i % 3
             for dx in range(3):
-                taps = [middle_ref[i * 9 + dx * 3 + dy] for dy in range(3)]
+                taps = [middle_ref[layer * 27 + tap_slice(dz) * 9 + dx * 3 + dy] for dy in range(3)]
                 wm[layer, pl.ds(pl.multiple_of(dz * 256 + dx * CH, CH), CH), 0:128] = jnp.concatenate([taps[0], taps[2]], axis=1)
                 wm[layer, pl.ds(pl.multiple_of(dz * 256 + dx * CH, CH), CH), 128:256] = jnp.concatenate([taps[1], taps[1]], axis=1)
             return carry
@@ -275,9 +280,98 @@
 
     phase_weights()
 
-    for copy in image_copies:
-        copy.wait()
+    for (r, _), copy in image_copies.items():
+        if r <= 1:
+            copy.wait()
     energy_copies = start_stage(0, 1, finish_stage(0, 0, energy_copies))
+    row24 = lax.broadcasted_iota(jnp.int32, (24, YP), 0) // 8 + (c - 1)
+
+    def feature_slice(zi):
+        slice_index = s + outward * (zi - 1)
+        valid = (row24 >= 0) & (row24 < 8) & (slice_index >= 0) & (slice_index < Z)
+        blocks = [halo[zi, k].astype(F32) for k in range(3)]
+        value = jnp.concatenate(
+            [jnp.concatenate([block[0:8], block[8:16, 0:128]], axis=1) for block in blocks], axis=0
+        )
+        value = jnp.where(valid, value, 0.0)
+        feats[0, zi] = lane_roll(value, 1)
+        feats[1, zi] = value
+        feats[2, zi] = lane_roll(value, -1)
+
+    lane = lax.broadcasted_iota(jnp.int32, (1, 256), 1)
+
+    def first_layer(z):
+        slice_index = s + outward * z
+        slice_valid = (slice_index >= 0) & (slice_index < Z)
+        columns = jnp.concatenate(
+            [feats[dy, z : z + 3].reshape(72, YP) for dy in range(3)] + [jnp.zeros((40, YP), F32)],
+            axis=0,
+        )
+        tall = jnp.transpose(columns)[0:Y].astype(BF16)
+        for x in range(0, 10, 2):
+            at = c * XB - 3 + x + lane // CH - lane // 128
+            mask = jnp.where((at >= 0) & (at < XW) & slice_valid, 1.0, 0.0)
+            product = dot(tall, w1[:, 128 * x : 128 * x + 256])
+            product = (jnp.maximum(product, 0.0) * mask).astype(BF16)
+            p1[z + 1, x] = product[:, 0:128]
+            p1[z + 1, x + 1] = product[:, 128:256]
+
+    low_lanes = lax.broadcasted_iota(jnp.int32, (Y, 128), 1) < CH
+
+    rowi = lax.broadcasted_iota(jnp.int32, (Y, 128), 0)
+    edge = jnp.where((low_lanes & (rowi == 0)) | (jnp.logical_not(low_lanes) & (rowi == Y - 1)), 0.0, 1.0)
+
+    def middle_slice(layer, source, target, rows, z, sent=()):
+        reach_x = (rows - XB) // 2
+        slice_index = s + outward * z
+        slice_valid = (slice_index >= 0) & (slice_index < Z)
+        before = None
+        for x in range(rows):
+            operand = jnp.concatenate(
+                [source[z + dz, x + 2 * k] for dz in range(3) for k in range(2)], axis=1
+            )
+            product = dot(operand, wm[layer])
+            at = c * XB - reach_x + x
+            mask = jnp.where((at >= 0) & (at < XW) & slice_valid, 1.0, 0.0).astype(F32)
+            first_half = product[:, 0:128]
+            outer = jnp.where(
+                low_lanes, pltpu.roll(first_half, 1, axis=0), pltpu.roll(first_half, Y - 1, axis=0)
+            )
+            outer = outer * edge
+            value = outer + lane_roll(outer, CH) + product[:, 128:256]
+            value = jnp.maximum(value, 0.0) * mask
+            if before is not None:
+                target[z + 1, x - 1] = jnp.where(low_lanes, before, value).astype(BF16)
+            before = value
+            for count, copy in sent:
+                if count == x:
+                    copy.start()
+        target[z + 1, rows - 1] = before.astype(BF16)
+        for count, copy in sent:
+            if count == rows:
+                copy.start()
+
+    def to_other_core(ref, blocks, index):
+        return pltpu.make_async_remote_copy(
+            src_ref=ref.at[1, blocks],
+            dst_ref=ref.at[0, blocks],
+            send_sem=core_send.at[index],
+            recv_sem=core_recv.at[index],
+            device_id=(s + 1 - 2 * core, c),
+            device_id_type=MESH,
+        )
+
+    first_copy = to_other_core(p1, pl.ds(0, 10), 0)
+    middle_copies = [(4, to_other_core(p2, pl.ds(0, 4), 1)), (8, to_other_core(p2, pl.ds(4, 4), 2))]
+    hidden_copies = [(x + 1, to_other_core(p3, pl.ds(x, 1), 3 + x // 2)) for x in (0, 2, 4)]
+
+    def phase_firstA():
+        for zi in range(3):
+            feature_slice(zi)
+        first_layer(0)
+
+    phase_firstA()
+    first_copy.start()
     map_copies = []
     for d in range(1, 8):
         target = (c + d) % 8
@@ -304,115 +398,57 @@
         )
         copy.start()
         rhs_copies.append(copy)
-
-    row24 = lax.broadcasted_iota(jnp.int32, (24, YP), 0) // 8 + (c - 1)
-
-    def feature_slice(zi, carry):
-        slice_index = s + zi - HALO
-        valid = (row24 >= 0) & (row24 < 8) & (slice_index >= 0) & (slice_index < Z)
-        blocks = [halo[zi, k].astype(F32) for k in range(3)]
-        value = jnp.concatenate(
-            [jnp.concatenate([block[0:8], block[8:16, 0:128]], axis=1) for block in blocks], axis=0
-        )
-        value = jnp.where(valid, value, 0.0)
-        feats[0, zi] = lane_roll(value, 1)
-        feats[1, zi] = value
-        feats[2, zi] = lane_roll(value, -1)
-        return carry
-
-    def phase_features():
-        for zi in range(2 * HALO + 1):
-            feature_slice(zi, 0)
-
-    phase_features()
-
-    lane = lax.broadcasted_iota(jnp.int32, (1, 256), 1)
-
-    def first_layer(z, carry):
-        slice_index = s + z - 3
-        slice_valid = (slice_index >= 0) & (slice_index < Z)
-        columns = jnp.concatenate(
-            [feats[dy, z : z + 3].reshape(72, YP) for dy in range(3)] + [jnp.zeros((40, YP), F32)],
-            axis=0,
-        )
-        tall = jnp.transpose(columns)[0:Y].astype(BF16)
-        for x in range(0, 10, 2):
-            at = c * XB - 3 + x + lane // CH - lane // 128
-            mask = jnp.where((at >= 0) & (at < XW) & slice_valid, 1.0, 0.0)
-            product = dot(tall, w1[:, 128 * x : 128 * x + 256])
-            product = (jnp.maximum(product, 0.0) * mask).astype(BF16)
-            p1[z, x] = product[:, 0:128]
-            p1[z, x + 1] = product[:, 128:256]
-        return carry
-
-    def phase_first():
-        for z in range(7):
-            first_layer(z, 0)
-
-    phase_first()
-
-    low_lanes = lax.broadcasted_iota(jnp.int32, (Y, 128), 1) < CH
-
-    rowi = lax.broadcasted_iota(jnp.int32, (Y, 128), 0)
-    edge = jnp.where((low_lanes & (rowi == 0)) | (jnp.logical_not(low_lanes) & (rowi == Y - 1)), 0.0, 1.0)
-
-    def middle_layer(layer, source, target, slices, rows, begin, end):
-        reach_z, reach_x = slices // 2, (rows - XB) // 2
-
-        def one_slice(z, carry):
-            slice_index = s + z - reach_z
-            slice_valid = (slice_index >= 0) & (slice_index < Z)
-            def finish(x, before):
-                at = c * XB - reach_x + x
-                mask = jnp.where((at >= 0) & (at < XW) & slice_valid, 1.0, 0.0).astype(F32)
-                first_half = products[x][:, 0:128]
-                outer = jnp.where(low_lanes, pltpu.roll(first_half, 1, axis=0), pltpu.roll(first_half, Y - 1, axis=0)) * edge
-                value = outer + lane_roll(outer, CH) + products[x][:, 128:256]
-                value = jnp.maximum(value, 0.0) * mask
-                if before is not None:
-                    target[z, x - 1] = jnp.where(low_lanes, before, value).astype(BF16)
-                return value
-
-            value = None
-            products = []
-            for x in range(0, rows + CHUNK, CHUNK):
-                if x < rows:
-                    operand = jnp.concatenate(
-                        [
-                            source[z + dz, x + 2 * k : x + 2 * k + CHUNK].reshape(CHUNK * Y, 128)
-                            for dz in range(3)
-                            for k in range(2)
-                        ],
-                        axis=1,
-                    )
-                    product = dot(operand, wm[layer])
-                    products.append(product)
-                if x > 0:
-                    for i in range(CHUNK):
-                        value = finish(x - CHUNK + i, value)
-            target[z, rows - 1] = value.astype(BF16)
-            return carry
-
-        lax.fori_loop(begin, end, one_slice, 0)
-
-    def phase_middle0():
-        middle_layer(0, p1, p2, 5, 8, 0, 3)
-
-    def phase_middle0b():
-        middle_layer(0, p1, p2, 5, 8, 3, 5)
-
-    phase_middle0()
+    for z in range(1, 4):
+        for dx in (-1, 0, 1):
+            image_copies[z + 1, dx].wait()
+        feature_slice(z + 2)
+        first_layer(z)
+
+    def phase_middleA():
+        middle_slice(0, p1, p2, 8, 2)
+
+    phase_middleA()
+    first_copy.wait()
+
+    def phase_middleB():
+        middle_slice(0, p1, p2, 8, 0, middle_copies)
+
+    phase_middleB()
     energy_copies = start_stage(0, 2, finish_stage(0, 1, energy_copies))
-    phase_middle0b()
-    def phase_middle1():
-        middle_layer(1, p2, p3, 3, 6, 0, 3)
-
-    phase_middle1()
+
+    def phase_middleC():
+        middle_slice(0, p1, p2, 8, 1)
+
+    phase_middleC()
+    for _, copy in middle_copies:
+        copy.wait()
+
+    def phase_hiddenA():
+        middle_slice(1, p2, p3, 6, 0, hidden_copies)
+
+    phase_hiddenA()
+
+    def phase_hiddenB():
+        middle_slice(1, p2, p3, 6, 1)
+
+    phase_hiddenB()
 
     def write(ref):
         for x in range(XB):
             for t, width in tiles:
                 ref[0, x, :, 128 * t : 128 * t + width] = pair[t, 2 * x : 2 * x + 2, 0:width]
+
+    for copy in map_copies:
+        copy.wait()
+
+    def phase_maps():
+        s_re, s_im = load_planes(lambda group, x: own_maps[group, x])
+        maps_re[...] = s_re
+        maps_im[...] = s_im
+
+    phase_maps()
+    for _, copy in hidden_copies:
+        copy.wait()
 
     def phase_last():
         operand = jnp.concatenate([p3[dz, 2 * k] for dz in range(3) for k in range(3)], axis=1)
@@ -441,15 +477,6 @@
         jnp.where(first_rows, adjoint, other) + reg * den_re,
         jnp.where(first_rows, other, adjoint) + reg * den_im,
     )
-    for copy in map_copies:
-        copy.wait()
-
-    def phase_maps():
-        s_re, s_im = load_planes(lambda group, x: own_maps[group, x])
-        maps_re[...] = s_re
-        maps_im[...] = s_im
-
-    phase_maps()
     energy = finish_stage(0, 2, energy_copies)
 
     mean = jnp.sum(energy, axis=1, keepdims=True) * (NS / Y / (Z * XW * Y))
@@ -550,9 +577,9 @@
         in_specs=[vmem, vmem, anywhere, anywhere, pl.BlockSpec(memory_space=pltpu.SMEM), vmem, vmem, vmem],
         out_specs=(vmem, vmem),
         scratch_shapes=[
-            pltpu.VMEM((9, 3, 16, 256), BF16),
+            pltpu.VMEM((6, 3, 16, 256), BF16),
             pltpu.VMEM((8, YP), F32),
-            pltpu.VMEM((3, 9, 24, YP), F32),
+            pltpu.VMEM((3, 6, 24, YP), F32),
             pltpu.VMEM((YP, 1280), F32),
             pltpu.VMEM((256, 1280), BF16),
             pltpu.VMEM((64, 128), F32),
@@ -560,8 +587,8 @@
             pltpu.VMEM((2, 768, 256), BF16),
             pltpu.VMEM((1152, 128), F32),
             pltpu.VMEM((1152, 128), BF16),
-            pltpu.VMEM((7, 10, Y, 128), BF16),
-            pltpu.VMEM((5, 8, Y, 128), BF16),
+            pltpu.VMEM((5, 10, Y, 128), BF16),
+            pltpu.VMEM((4, 8, Y, 128), BF16),
             pltpu.VMEM((3, 6, Y, 128), BF16),
             pltpu.VMEM((2 * YP, 256), BF16),
             pltpu.VMEM((2 * YP, 256), BF16),
@@ -578,8 +605,8 @@
             pltpu.VMEM((3, 16, 128), F32),
             pltpu.VMEM((8, 128), F32),
             pltpu.VMEM((2, 3, 8, 1, 128), F32),
-            dma((3,)), dma((26,)), dma((26,)), dma((7,)), dma((7,)), dma((7,)), dma((7,)),
-            dma((2, 3, 7)), dma((2, 3, 7)),
+            dma((3,)), dma((17,)), dma((17,)), dma((7,)), dma((7,)), dma((7,)), dma((7,)),
+            dma((2, 3, 7)), dma((2, 3, 7)), dma((6,)), dma((6,)),
         ],
         compiler_params=pltpu.CompilerParams(
             collective_id=0, has_side_effects=True, vmem_limit_bytes=LIMIT

time: 56.5 us -> 51.9 us (0.919)
  Pallas kernels: 52.2 us -> 47.6 us
    pallas_call x1, Pallas kernels: 52.2 us -> 47.6 us  [local(): pl.pallas_call(kernel, out_shape=(block, block), in_specs=[vmem, vmem, an...]
where the time goes in v4:
time: 51.9 us; the launch traced here: 50.9 us
  Pallas kernels  47.6 us (92%)
  local copies, waits for them, and re-layouts  1.92 us (4%)
  between operations  1.29 us (2%)
    pallas_call x1, Pallas kernels, local(): pl.pallas_call(kernel, out_shape=(block, block), in_specs=[vmem, vmem, an...  47.6 us
    unnamed x4, local copies, waits for them, and re-layouts  1.92 us

profile of v4, /device:TPU:1, one launch (start us, length us, event | category | flops | bytes accessed | tf_op | source)
XLA Modules:
  0.0 50.9 jit_solution(17556066759558902337)
XLA Ops:
  1.3 47.6 %shard_map.95 = (f32[1,4,2,320]{3,2,1,0:T(2,128)}, f32[1,4,2,320]{3,2,1,0:T(2,128)}) custom-call(f32[1,4,2,320]{3,2,1,0:T(2,128)} %image_ref.1, s32[1,80]{1,0:T(1,128)} %lines_ref.1, f32[4,1,32,2,320]{4,3,2,1,0:T(2,128)} %maps_hbm.1, f32[4,1,32,2,320]{4,3,2,1,0:T(2,128)} %kspace_hbm.1, f32[1]{0:T(128)S(6)} %copy.12.reg_ref, bf16[27,2,64]{2,1,0:T(2,128)(2,1)} %bitcast.6, ...), custom_call_target="tpu_custom_call" | custom-call | tf_op jit(solution)/shard_map/pallas_call | solution.py:574
  48.9 0.0 copy-start
  48.9 1.3 %copy.13 = f32[1,4,2,320]{3,2,1,0:T(2,128)} copy(f32[1,4,2,320]{3,2,1,0:T(2,128)} %get-tuple-element.4) | data formatting | bytes 20480
  50.3 0.0 copy-done
  50.3 0.6 %copy.14 = f32[1,4,2,320]{3,2,1,0:T(2,128)} copy(f32[1,4,2,320]{3,2,1,0:T(2,128)S(1)} %copy-done) | data formatting | bytes 20480
Async XLA Ops:
  48.9 1.3 %copy-start = (f32[1,4,2,320]{3,2,1,0:T(2,128)S(1)}, f32[1,4,2,320]{3,2,1,0:T(2,128)}, u32[]{:S(2)}) copy-start(f32[1,4,2,320]{3,2,1,0:T(2,128)} %get-tuple-element.5) | copy-start | bytes 30724

commit v5 on v4

--- a/solution.py
+++ b/solution.py
@@ -53,8 +53,9 @@
 
 
 def kernel(
-    image_ref, lines_ref, maps_hbm, kspace_hbm, reg_ref, first_ref, middle_ref, last_ref,
+    image_hbm, lines_hbm, maps_hbm, kspace_hbm, reg_hbm, first_hbm, middle_hbm, last_hbm,
     denoised_ref, out_ref,
+    image_ref, lines_ref, reg_ref, first_ref, middle_ref, last_ref,
     halo, own_image, feats, w1f, w1, wt, wl, wm, w4f, w4, p1, p2, p3,
     table_hi, table_lo, pick, local_maps, local_kspace, own_maps, inter, planes, maps_re, maps_im,
     part_send, part_recv, pair, energy_out, slots,
@@ -94,6 +95,21 @@
     for partner in partners:
         pl.semaphore_signal(barrier, inc=1, device_id=partner, device_id_type=MESH)
 
+    image_in, lines_in, reg_in, first_in, middle_in, last_in = [
+        pltpu.make_async_copy(source, target, local_sem.at[3 + i])
+        for i, (source, target) in enumerate(
+            (
+                (image_hbm, image_ref),
+                (lines_hbm, lines_ref),
+                (reg_hbm, reg_ref),
+                (first_hbm, first_ref),
+                (middle_hbm, middle_ref),
+                (last_hbm, last_ref),
+            )
+        )
+    ]
+    for copy in (image_in, lines_in, first_in, last_in, reg_in):
+        copy.start()
     local_copies = [
         pltpu.make_async_copy(maps_hbm.at[:, 0], local_maps, local_sem.at[0]),
         pltpu.make_async_copy(kspace_hbm.at[:, 0], local_kspace, local_sem.at[1]),
@@ -103,8 +119,10 @@
     ]
     for copy in local_copies:
         copy.start()
+    middle_in.start()
 
     own_image[...] = jnp.zeros_like(own_image)
+    image_in.wait()
     for x in range(XB):
         own_image[2 * x : 2 * x + 2, 0:Y] = image_ref[0, x]
     mine = own_image[...]
@@ -125,6 +143,8 @@
         )
         copy.start()
         image_copies[r, dx] = copy
+    lines_in.wait()
+
     def phase_tables():
         lines = jnp.concatenate([lines_ref[...], jnp.full((1, 128 - NS), -1, jnp.int32)], axis=1)
         position = lax.broadcasted_iota(jnp.int32, (YP, 128), 0)
@@ -230,6 +250,9 @@
         for k in range(27):
             wl[2 * k : 2 * k + 2, 0:CH] = last_ref[tap_slice(k // 9) * 9 + k % 9].astype(F32)
         return wl[...]
+
+    for copy in (first_in, middle_in, last_in, reg_in):
+        copy.wait()
 
     def phase_weights():
         wt[...] = jnp.zeros_like(wt)
@@ -525,58 +548,67 @@
     moments = phase_krylov()
     for stage in range(3):
         moments = finish_stage(1, stage, start_stage(1, stage, moments))
-    place = lax.broadcasted_iota(jnp.int32, (1, 128), 1) // 8
-    values = [
-        jnp.sum(jnp.where(place == i, moments, 0.0), axis=1, keepdims=True) for i in range(len(pairs) + 1)
-    ]
-    gram = {}
-    for row, (i, j) in enumerate(pairs):
-        gram[i, j] = gram[j, i] = values[row]
-    shift = mean + reg
-    matrix = {}
-    for i in range(4):
-        for j in range(i, 4):
-            value = gram[i + 1, j] + shift * gram[i, j] if i < 3 else values[10] + reg * gram[3, 3]
-            matrix[i, j] = matrix[j, i] = value
-    norm = [jnp.where(matrix[i, i] > 1e-37, lax.rsqrt(jnp.maximum(matrix[i, i], 1e-37)), 0.0) for i in range(4)]
-    side = [gram[0, i] * norm[i] for i in range(4)]
-    for i in range(4):
-        for j in range(i, 4):
-            matrix[i, j] = matrix[j, i] = matrix[i, j] * norm[i] * norm[j]
-    inverse = []
-    for k in range(4):
-        pivot = matrix[k, k]
-        inverse.append(jnp.where(pivot > 2e-6, 1.0 / jnp.maximum(pivot, 2e-6), 0.0))
-        for i in range(k + 1, 4):
-            factor = matrix[i, k] * inverse[k]
+    def phase_solve():
+        place = lax.broadcasted_iota(jnp.int32, (1, 128), 1) // 8
+        values = [
+            jnp.sum(jnp.where(place == i, moments, 0.0), axis=1, keepdims=True) for i in range(len(pairs) + 1)
+        ]
+        gram = {}
+        for row, (i, j) in enumerate(pairs):
+            gram[i, j] = gram[j, i] = values[row]
+        shift = mean + reg
+        matrix = {}
+        for i in range(4):
             for j in range(i, 4):
-                matrix[i, j] = matrix[j, i] = matrix[i, j] - factor * matrix[k, j]
-            side[i] = side[i] - factor * side[k]
-    weights = [None] * 4
-    for k in range(3, -1, -1):
-        value = side[k]
-        for j in range(k + 1, 4):
-            value = value - matrix[k, j] * weights[j]
-        weights[k] = value * inverse[k]
-    real = sum(weights[k] * norm[k] * basis[k][0] for k in range(4))
-    imag = sum(weights[k] * norm[k] * basis[k][1] for k in range(4))
-    for t in range(3):
-        pair[t, pl.ds(0, 8, stride=2), :] = real[:, 128 * t : 128 * t + 128]
-        pair[t, pl.ds(1, 8, stride=2), :] = imag[:, 128 * t : 128 * t + 128]
-    write(out_ref)
+                value = gram[i + 1, j] + shift * gram[i, j] if i < 3 else values[10] + reg * gram[3, 3]
+                matrix[i, j] = matrix[j, i] = value
+        norm = [jnp.where(matrix[i, i] > 1e-37, lax.rsqrt(jnp.maximum(matrix[i, i], 1e-37)), 0.0) for i in range(4)]
+        side = [gram[0, i] * norm[i] for i in range(4)]
+        for i in range(4):
+            for j in range(i, 4):
+                matrix[i, j] = matrix[j, i] = matrix[i, j] * norm[i] * norm[j]
+        inverse = []
+        for k in range(4):
+            pivot = matrix[k, k]
+            inverse.append(jnp.where(pivot > 2e-6, 1.0 / jnp.maximum(pivot, 2e-6), 0.0))
+            for i in range(k + 1, 4):
+                factor = matrix[i, k] * inverse[k]
+                for j in range(i, 4):
+                    matrix[i, j] = matrix[j, i] = matrix[i, j] - factor * matrix[k, j]
+                side[i] = side[i] - factor * side[k]
+        weights = [None] * 4
+        for k in range(3, -1, -1):
+            value = side[k]
+            for j in range(k + 1, 4):
+                value = value - matrix[k, j] * weights[j]
+            weights[k] = value * inverse[k]
+        real = sum(weights[k] * norm[k] * basis[k][0] for k in range(4))
+        imag = sum(weights[k] * norm[k] * basis[k][1] for k in range(4))
+        for t in range(3):
+            pair[t, pl.ds(0, 8, stride=2), :] = real[:, 128 * t : 128 * t + 128]
+            pair[t, pl.ds(1, 8, stride=2), :] = imag[:, 128 * t : 128 * t + 128]
+        write(out_ref)
+
+    phase_solve()
 
 
 def local(image, sampled_lines, coil_maps, kspace, reg_weight, conv_first, conv_middle, conv_last):
     vmem = pl.BlockSpec(memory_space=pltpu.VMEM)
-    anywhere = pl.BlockSpec(memory_space=pl.ANY)
-    block = jax.ShapeDtypeStruct((1, XB, 2, Y), F32)
+    anywhere = pl.BlockSpec(memory_space=pltpu.HBM)
+    block = pltpu.VMEM((1, XB, 2, Y), F32)
     dma = pltpu.SemaphoreType.DMA
     return pl.pallas_call(
         kernel,
         out_shape=(block, block),
-        in_specs=[vmem, vmem, anywhere, anywhere, pl.BlockSpec(memory_space=pltpu.SMEM), vmem, vmem, vmem],
+        in_specs=[anywhere] * 8,
         out_specs=(vmem, vmem),
         scratch_shapes=[
+            pltpu.VMEM((1, XB, 2, Y), F32),
+            pltpu.VMEM((1, NS), jnp.int32),
+            pltpu.SMEM((1,), F32),
+            pltpu.VMEM((27, 2, CH), BF16),
+            pltpu.VMEM((54, CH, CH), BF16),
+            pltpu.VMEM((27, 2, CH), BF16),
             pltpu.VMEM((6, 3, 16, 256), BF16),
             pltpu.VMEM((8, YP), F32),
             pltpu.VMEM((3, 6, 24, YP), F32),
@@ -605,7 +637,7 @@
             pltpu.VMEM((3, 16, 128), F32),
             pltpu.VMEM((8, 128), F32),
             pltpu.VMEM((2, 3, 8, 1, 128), F32),
-            dma((3,)), dma((17,)), dma((17,)), dma((7,)), dma((7,)), dma((7,)), dma((7,)),
+            dma((9,)), dma((17,)), dma((17,)), dma((7,)), dma((7,)), dma((7,)), dma((7,)),
             dma((2, 3, 7)), dma((2, 3, 7)), dma((6,)), dma((6,)),
         ],
         compiler_params=pltpu.CompilerParams(

time: 51.9 us -> 49.6 us (0.956)
  Pallas kernels: 47.6 us -> 46.2 us
  local copies, waits for them, and re-layouts: 1.92 us -> 1.2 us
    pallas_call x1, Pallas kernels: 47.6 us -> 46.2 us  [local(): pl.pallas_call(kernel, out_shape=(block, block), in_specs=[anywhere] * 8,...]
    unnamed x4 -> x2, local copies, waits for them, and re-layouts: 1.92 us -> 1.2 us
where the time goes in v5:
time: 49.6 us; the launch traced here: 48.7 us
  Pallas kernels  46.2 us (93%)
  between operations  1.29 us (3%)
  local copies, waits for them, and re-layouts  1.2 us (2%)
    pallas_call x1, Pallas kernels, local(): pl.pallas_call(kernel, out_shape=(block, block), in_specs=[anywhere] * 8,...  46.2 us
    unnamed x2, local copies, waits for them, and re-layouts  1.2 us

profile of v5, /device:TPU:1, one launch (start us, length us, event | category | flops | bytes accessed | tf_op | source)
XLA Modules:
  0.0 48.7 jit_solution(14572784129535806143)
XLA Ops:
  1.3 46.2 %shard_map.95 = (f32[1,4,2,320]{3,2,1,0:T(2,128)S(1)}, f32[1,4,2,320]{3,2,1,0:T(2,128)S(1)}) custom-call(f32[1,4,2,320]{3,2,1,0:T(2,128)} %image_hbm.1, s32[1,80]{1,0:T(1,128)} %lines_hbm.1, f32[4,1,32,2,320]{4,3,2,1,0:T(2,128)} %maps_hbm.1, f32[4,1,32,2,320]{4,3,2,1,0:T(2,128)} %kspace_hbm.1, f32[1]{0:T(128)S(6)} %copy.14.reg_hbm, ...), custom_call_target="tpu_custom_call" | custom-call | tf_op jit(solution)/shard_map/pallas_call | solution.py:600
  47.4 0.6 %copy.12 = f32[1,4,2,320]{3,2,1,0:T(2,128)} copy(f32[1,4,2,320]{3,2,1,0:T(2,128)S(1)} %get-tuple-element.2) | data formatting | bytes 20480
  48.1 0.6 %copy.13 = f32[1,4,2,320]{3,2,1,0:T(2,128)} copy(f32[1,4,2,320]{3,2,1,0:T(2,128)S(1)} %get-tuple-element.3) | data formatting | bytes 20480

commit v6 on v5

--- a/solution.py
+++ b/solution.py
@@ -69,7 +69,7 @@
     z_chip = z_hi * 2 + z_lo
 
     outward = 2 * core - 1
-    offsets = [(r, dx) for r in range(-1, HALO + 1) for dx in (-1, 0, 1) if (r, dx) != (0, 0)]
+    offsets = [(r, dx) for r in (4, 3, 1, 2, 0, -1) for dx in (-1, 1, 0) if (r, dx) != (0, 0)]
 
     def needing(r, dx):
         away = r if r % 2 == 0 else -r
@@ -87,13 +87,6 @@
         return ((z_new // 2) * 16 + y_chip * 2 + core, (z_new % 2) * 4 + x_chip)
 
     stage_index = (core * 4 + x_chip, y_chip, z_chip)
-
-    partners = [((s + outward * r + Z) % Z, (c + dx + 8) % 8) for r, dx in offsets]
-    partners += [(s, (c + d) % 8) for d in range(1, 8)]
-    partners += [stage_partner(stage, d) for stage in range(3) for d in range(1, 8)]
-    barrier = pltpu.get_barrier_semaphore()
-    for partner in partners:
-        pl.semaphore_signal(barrier, inc=1, device_id=partner, device_id_type=MESH)
 
     image_in, lines_in, reg_in, first_in, middle_in, last_in = [
         pltpu.make_async_copy(source, target, local_sem.at[3 + i])
@@ -108,7 +101,16 @@
             )
         )
     ]
-    for copy in (image_in, lines_in, first_in, last_in, reg_in):
+    image_in.start()
+
+    partners = [((s + outward * r + Z) % Z, (c + dx + 8) % 8) for r, dx in offsets]
+    partners += [(s, (c + d) % 8) for d in range(1, 8)]
+    partners += [stage_partner(stage, d) for stage in range(3) for d in range(1, 8)]
+    barrier = pltpu.get_barrier_semaphore()
+    for partner in partners:
+        pl.semaphore_signal(barrier, inc=1, device_id=partner, device_id_type=MESH)
+
+    for copy in (lines_in, first_in, last_in, reg_in):
         copy.start()
     local_copies = [
         pltpu.make_async_copy(maps_hbm.at[:, 0], local_maps, local_sem.at[0]),
@@ -592,12 +594,23 @@
     phase_solve()
 
 
+def write_out(first, second, first_out, second_out, sems):
+    copies = [
+        pltpu.make_async_copy(first, first_out, sems.at[0]),
+        pltpu.make_async_copy(second, second_out, sems.at[1]),
+    ]
+    for copy in copies:
+        copy.start()
+    for copy in copies:
+        copy.wait()
+
+
 def local(image, sampled_lines, coil_maps, kspace, reg_weight, conv_first, conv_middle, conv_last):
     vmem = pl.BlockSpec(memory_space=pltpu.VMEM)
     anywhere = pl.BlockSpec(memory_space=pltpu.HBM)
     block = pltpu.VMEM((1, XB, 2, Y), F32)
     dma = pltpu.SemaphoreType.DMA
-    return pl.pallas_call(
+    results = pl.pallas_call(
         kernel,
         out_shape=(block, block),
         in_specs=[anywhere] * 8,
@@ -647,6 +660,14 @@
         image, sampled_lines, coil_maps, kspace, reg_weight,
         conv_first.reshape(27, 2, CH), conv_middle.reshape(54, CH, CH), conv_last.transpose(0, 1, 2, 4, 3).reshape(27, 2, CH),
     )
+    hbm = pl.BlockSpec(memory_space=pltpu.HBM)
+    return pl.pallas_call(
+        write_out,
+        out_shape=(jax.ShapeDtypeStruct((1, XB, 2, Y), F32),) * 2,
+        in_specs=[vmem, vmem],
+        out_specs=(hbm, hbm),
+        scratch_shapes=[dma((2,))],
+    )(*results)
 
 
 def solution(mesh):

time: 49.6 us -> 51.3 us (1.034)
  the two profiles are of different devices: /device:TPU:1 before, /device:TPU:8 now
where the time goes in v6:
time: 51.3 us; the launch traced here: 51 us
  Pallas kernels  48.5 us (95%)
  between operations  1.29 us (3%)
  local copies, waits for them, and re-layouts  1.18 us (2%)
    pallas_call x1, Pallas kernels, local(): pl.pallas_call(kernel, out_shape=(block, block), in_specs=[anywhere] * 8,...  47.2 us
    pallas_call x1, Pallas kernels, local(): pl.pallas_call(write_out, out_shape=(jax.ShapeDtypeStruct((1, XB, 2, Y),...  1.34 us
    unnamed x4, local copies, waits for them, and re-layouts  1.18 us

profile of v6, /device:TPU:8, one launch (start us, length us, event | category | flops | bytes accessed | tf_op | source)
XLA Modules:
  0.0 51.0 jit_solution(2912716415873736623)
XLA Ops:
  1.3 47.2 %shard_map.95 = (f32[1,4,2,320]{3,2,1,0:T(2,128)S(1)}, f32[1,4,2,320]{3,2,1,0:T(2,128)S(1)}) custom-call(f32[1,4,2,320]{3,2,1,0:T(2,128)} %image_hbm.1, s32[1,80]{1,0:T(1,128)} %lines_hbm.1, f32[4,1,32,2,320]{4,3,2,1,0:T(2,128)} %maps_hbm.1, f32[4,1,32,2,320]{4,3,2,1,0:T(2,128)} %kspace_hbm.1, f32[1]{0:T(128)S(6)} %copy.10.reg_hbm, ...), custom_call_target="tpu_custom_call" | custom-call | tf_op jit(solution)/shard_map/pallas_call | solution.py:613
  48.5 0.0 copy-start
  48.5 0.6 %copy-done = f32[1,4,2,320]{3,2,1,0:T(2,128)} copy-done((f32[1,4,2,320]{3,2,1,0:T(2,128)}, f32[1,4,2,320]{3,2,1,0:T(2,128)S(1)}, u32[]{:S(2)}) %copy-start) | copy-done | bytes 10264
  49.1 0.0 copy-start.1
  49.1 0.6 %copy-done.1 = f32[1,4,2,320]{3,2,1,0:T(2,128)} copy-done((f32[1,4,2,320]{3,2,1,0:T(2,128)}, f32[1,4,2,320]{3,2,1,0:T(2,128)S(1)}, u32[]{:S(2)}) %copy-start.1) | copy-done | bytes 10264
  49.7 1.3 %shard_map.96 = (f32[1,4,2,320]{3,2,1,0:T(2,128)}, f32[1,4,2,320]{3,2,1,0:T(2,128)}) custom-call(f32[1,4,2,320]{3,2,1,0:T(2,128)} %copy-done, f32[1,4,2,320]{3,2,1,0:T(2,128)} %copy-done.1), custom_call_target="tpu_custom_call" | custom-call | tf_op jit(solution)/shard_map/pallas_call | solution.py:664
Async XLA Ops:
  48.5 0.6 %copy-start = (f32[1,4,2,320]{3,2,1,0:T(2,128)}, f32[1,4,2,320]{3,2,1,0:T(2,128)S(1)}, u32[]{:S(2)}) copy-start(f32[1,4,2,320]{3,2,1,0:T(2,128)S(1)} %get-tuple-element.4.first) | copy-start | bytes 30724
  49.1 0.6 %copy-start.1 = (f32[1,4,2,320]{3,2,1,0:T(2,128)}, f32[1,4,2,320]{3,2,1,0:T(2,128)S(1)}, u32[]{:S(2)}) copy-start(f32[1,4,2,320]{3,2,1,0:T(2,128)S(1)} %get-tuple-element.5.second) | copy-start | bytes 30724

commit v7 on v5

--- a/solution.py
+++ b/solution.py
@@ -57,7 +57,7 @@
     denoised_ref, out_ref,
     image_ref, lines_ref, reg_ref, first_ref, middle_ref, last_ref,
     halo, own_image, feats, w1f, w1, wt, wl, wm, w4f, w4, p1, p2, p3,
-    table_hi, table_lo, pick, local_maps, local_kspace, own_maps, inter, planes, maps_re, maps_im,
+    table_hi, table_lo, back_hi, back_lo, pick, local_maps, local_kspace, own_maps, inter, planes, maps_re, maps_im,
     part_send, part_recv, pair, energy_out, slots,
     local_sem, img_send, img_recv, map_send, map_recv, rhs_send, rhs_recv, sum_send, sum_recv,
     core_send, core_recv,
@@ -69,7 +69,7 @@
     z_chip = z_hi * 2 + z_lo
 
     outward = 2 * core - 1
-    offsets = [(r, dx) for r in range(-1, HALO + 1) for dx in (-1, 0, 1) if (r, dx) != (0, 0)]
+    offsets = [(r, dx) for r in (4, 3, 1, 2, 0, -1) for dx in (-1, 1, 0) if (r, dx) != (0, 0)]
 
     def needing(r, dx):
         away = r if r % 2 == 0 else -r
@@ -87,13 +87,6 @@
         return ((z_new // 2) * 16 + y_chip * 2 + core, (z_new % 2) * 4 + x_chip)
 
     stage_index = (core * 4 + x_chip, y_chip, z_chip)
-
-    partners = [((s + outward * r + Z) % Z, (c + dx + 8) % 8) for r, dx in offsets]
-    partners += [(s, (c + d) % 8) for d in range(1, 8)]
-    partners += [stage_partner(stage, d) for stage in range(3) for d in range(1, 8)]
-    barrier = pltpu.get_barrier_semaphore()
-    for partner in partners:
-        pl.semaphore_signal(barrier, inc=1, device_id=partner, device_id_type=MESH)
 
     image_in, lines_in, reg_in, first_in, middle_in, last_in = [
         pltpu.make_async_copy(source, target, local_sem.at[3 + i])
@@ -108,7 +101,16 @@
             )
         )
     ]
-    for copy in (image_in, lines_in, first_in, last_in, reg_in):
+    image_in.start()
+
+    partners = [((s + outward * r + Z) % Z, (c + dx + 8) % 8) for r, dx in offsets]
+    partners += [(s, (c + d) % 8) for d in range(1, 8)]
+    partners += [stage_partner(stage, d) for stage in range(3) for d in range(1, 8)]
+    barrier = pltpu.get_barrier_semaphore()
+    for partner in partners:
+        pl.semaphore_signal(barrier, inc=1, device_id=partner, device_id_type=MESH)
+
+    for copy in (lines_in, first_in, last_in, reg_in):
         copy.start()
     local_copies = [
         pltpu.make_async_copy(maps_hbm.at[:, 0], local_maps, local_sem.at[0]),
@@ -172,6 +174,12 @@
             high, low = split(value)
             table_hi[row : row + YP, column : column + 128] = high
             table_lo[row : row + YP, column : column + 128] = low
+        for row, column, value in (
+            (0, 0, cosine), (128, 0, -sine), (0, YP, sine), (128, YP, cosine),
+        ):
+            high, low = split(jnp.transpose(value))
+            back_hi[row : row + 128, column : column + YP] = high
+            back_lo[row : row + 128, column : column + YP] = low
         pick[...] = jnp.where(inside & (position == line), 1.0, 0.0).astype(BF16)
 
     phase_tables()
@@ -203,7 +211,7 @@
         for plane in (kspace_re, kspace_im):
             high, low = split(plane)
             spectrum.append(dot(high, pick[...]) + dot(low, pick[...]))
-        field = dot3(jnp.concatenate(spectrum, axis=1), table_hi, table_lo, dot_t)
+        field = dot3(jnp.concatenate(spectrum, axis=1), back_hi, back_lo, dot)
         planes[...] = field
         s_re, s_im = load_planes(lambda group, x: local_maps[group // 8, (group % 8) * XB + x])
         energy = s_re * s_re + s_im * s_im
@@ -302,11 +310,37 @@
         w4[...] = w4f[...].astype(BF16)
 
     phase_weights()
+    rhs_copies = []
+    for d in range(1, 8):
+        target = (c + d) % 8
+        copy = pltpu.make_async_remote_copy(
+            src_ref=part_send.at[target],
+            dst_ref=part_recv.at[c],
+            send_sem=rhs_send.at[d - 1],
+            recv_sem=rhs_recv.at[d - 1],
+            device_id=(s, target),
+            device_id_type=MESH,
+        )
+        copy.start()
+        rhs_copies.append(copy)
+    energy_copies = start_stage(0, 1, finish_stage(0, 0, energy_copies))
 
     for (r, _), copy in image_copies.items():
         if r <= 1:
             copy.wait()
-    energy_copies = start_stage(0, 1, finish_stage(0, 0, energy_copies))
+    map_copies = []
+    for d in range(1, 8):
+        target = (c + d) % 8
+        copy = pltpu.make_async_remote_copy(
+            src_ref=maps_hbm.at[:, 0, pl.ds(target * XB, XB)],
+            dst_ref=own_maps.at[pl.ds(c * CL, CL)],
+            send_sem=map_send.at[d - 1],
+            recv_sem=map_recv.at[d - 1],
+            device_id=(s, target),
+            device_id_type=MESH,
+        )
+        copy.start()
+        map_copies.append(copy)
     row24 = lax.broadcasted_iota(jnp.int32, (24, YP), 0) // 8 + (c - 1)
 
     def feature_slice(zi):
@@ -395,37 +429,12 @@
 
     phase_firstA()
     first_copy.start()
-    map_copies = []
-    for d in range(1, 8):
-        target = (c + d) % 8
-        copy = pltpu.make_async_remote_copy(
-            src_ref=maps_hbm.at[:, 0, pl.ds(target * XB, XB)],
-            dst_ref=own_maps.at[pl.ds(c * CL, CL)],
-            send_sem=map_send.at[d - 1],
-            recv_sem=map_recv.at[d - 1],
-            device_id=(s, target),
-            device_id_type=MESH,
-        )
-        copy.start()
-        map_copies.append(copy)
-    rhs_copies = []
-    for d in range(1, 8):
-        target = (c + d) % 8
-        copy = pltpu.make_async_remote_copy(
-            src_ref=part_send.at[target],
-            dst_ref=part_recv.at[c],
-            send_sem=rhs_send.at[d - 1],
-            recv_sem=rhs_recv.at[d - 1],
-            device_id=(s, target),
-            device_id_type=MESH,
-        )
-        copy.start()
-        rhs_copies.append(copy)
     for z in range(1, 4):
         for dx in (-1, 0, 1):
             image_copies[z + 1, dx].wait()
         feature_slice(z + 2)
         first_layer(z)
+    energy_copies = start_stage(0, 2, finish_stage(0, 1, energy_copies))
 
     def phase_middleA():
         middle_slice(0, p1, p2, 8, 2)
@@ -437,7 +446,6 @@
         middle_slice(0, p1, p2, 8, 0, middle_copies)
 
     phase_middleB()
-    energy_copies = start_stage(0, 2, finish_stage(0, 1, energy_copies))
 
     def phase_middleC():
         middle_slice(0, p1, p2, 8, 1)
@@ -512,7 +520,7 @@
         return dot3(weighted, table_hi, table_lo, dot)
 
     def gram_map(vector):
-        planes[...] = dot3(spectrum_of(vector), table_hi, table_lo, dot_t)
+        planes[...] = dot3(spectrum_of(vector), back_hi, back_lo, dot)
         m_re, m_im = maps_re[...], maps_im[...]
         f_re, f_im = planes[:, 0:YP], planes[:, YP : 2 * YP]
         real = jnp.sum((m_re * f_re + m_im * f_im).reshape(16, 8, YP), axis=0)
@@ -624,6 +632,8 @@
             pltpu.VMEM((3, 6, Y, 128), BF16),
             pltpu.VMEM((2 * YP, 256), BF16),
             pltpu.VMEM((2 * YP, 256), BF16),
+            pltpu.VMEM((256, 2 * YP), BF16),
+            pltpu.VMEM((256, 2 * YP), BF16),
             pltpu.VMEM((YP, 128), BF16),
             pltpu.VMEM((CL, XW, 2, Y), F32),
             pltpu.VMEM((CL, XW, 2, Y), F32),

time: 49.6 us -> 51.8 us (1.044)
  Pallas kernels: 46.2 us -> 48.3 us
    pallas_call x1, Pallas kernels: 46.2 us -> 48.3 us  [local(): pl.pallas_call(kernel, out_shape=(block, block), in_specs=[anywhere] * 8,...]
where the time goes in v7:
time: 51.8 us; the launch traced here: 50.8 us
  Pallas kernels  48.3 us (93%)
  between operations  1.29 us (2%)
  local copies, waits for them, and re-layouts  1.2 us (2%)
    pallas_call x1, Pallas kernels, local(): pl.pallas_call(kernel, out_shape=(block, block), in_specs=[anywhere] * 8,...  48.3 us
    unnamed x2, local copies, waits for them, and re-layouts  1.2 us

profile of v7, /device:TPU:1, one launch (start us, length us, event | category | flops | bytes accessed | tf_op | source)
XLA Modules:
  0.0 50.8 jit_solution(4496619964835763934)
XLA Ops:
  1.3 48.3 %shard_map.95 = (f32[1,4,2,320]{3,2,1,0:T(2,128)S(1)}, f32[1,4,2,320]{3,2,1,0:T(2,128)S(1)}) custom-call(f32[1,4,2,320]{3,2,1,0:T(2,128)} %image_hbm.1, s32[1,80]{1,0:T(1,128)} %lines_hbm.1, f32[4,1,32,2,320]{4,3,2,1,0:T(2,128)} %maps_hbm.1, f32[4,1,32,2,320]{4,3,2,1,0:T(2,128)} %kspace_hbm.1, f32[1]{0:T(128)S(6)} %copy.14.reg_hbm, ...), custom_call_target="tpu_custom_call" | custom-call | tf_op jit(solution)/shard_map/pallas_call | solution.py:608
  49.6 0.6 %copy.12 = f32[1,4,2,320]{3,2,1,0:T(2,128)} copy(f32[1,4,2,320]{3,2,1,0:T(2,128)S(1)} %get-tuple-element.2) | data formatting | bytes 20480
  50.2 0.6 %copy.13 = f32[1,4,2,320]{3,2,1,0:T(2,128)} copy(f32[1,4,2,320]{3,2,1,0:T(2,128)S(1)} %get-tuple-element.3) | data formatting | bytes 20480

commit v8 on v5

--- a/solution.py
+++ b/solution.py
@@ -57,7 +57,7 @@
     denoised_ref, out_ref,
     image_ref, lines_ref, reg_ref, first_ref, middle_ref, last_ref,
     halo, own_image, feats, w1f, w1, wt, wl, wm, w4f, w4, p1, p2, p3,
-    table_hi, table_lo, pick, local_maps, local_kspace, own_maps, inter, planes, maps_re, maps_im,
+    table_hi, table_lo, back_hi, back_lo, pick, local_maps, local_kspace, own_maps, inter, planes, maps_re, maps_im,
     part_send, part_recv, pair, energy_out, slots,
     local_sem, img_send, img_recv, map_send, map_recv, rhs_send, rhs_recv, sum_send, sum_recv,
     core_send, core_recv,
@@ -69,7 +69,7 @@
     z_chip = z_hi * 2 + z_lo
 
     outward = 2 * core - 1
-    offsets = [(r, dx) for r in range(-1, HALO + 1) for dx in (-1, 0, 1) if (r, dx) != (0, 0)]
+    offsets = [(r, dx) for r in (4, 3, 1, 2, 0, -1) for dx in (-1, 1, 0) if (r, dx) != (0, 0)]
 
     def needing(r, dx):
         away = r if r % 2 == 0 else -r
@@ -87,13 +87,6 @@
         return ((z_new // 2) * 16 + y_chip * 2 + core, (z_new % 2) * 4 + x_chip)
 
     stage_index = (core * 4 + x_chip, y_chip, z_chip)
-
-    partners = [((s + outward * r + Z) % Z, (c + dx + 8) % 8) for r, dx in offsets]
-    partners += [(s, (c + d) % 8) for d in range(1, 8)]
-    partners += [stage_partner(stage, d) for stage in range(3) for d in range(1, 8)]
-    barrier = pltpu.get_barrier_semaphore()
-    for partner in partners:
-        pl.semaphore_signal(barrier, inc=1, device_id=partner, device_id_type=MESH)
 
     image_in, lines_in, reg_in, first_in, middle_in, last_in = [
         pltpu.make_async_copy(source, target, local_sem.at[3 + i])
@@ -108,7 +101,16 @@
             )
         )
     ]
-    for copy in (image_in, lines_in, first_in, last_in, reg_in):
+    image_in.start()
+
+    partners = [((s + outward * r + Z) % Z, (c + dx + 8) % 8) for r, dx in offsets]
+    partners += [(s, (c + d) % 8) for d in range(1, 8)]
+    partners += [stage_partner(stage, d) for stage in range(3) for d in range(1, 8)]
+    barrier = pltpu.get_barrier_semaphore()
+    for partner in partners:
+        pl.semaphore_signal(barrier, inc=1, device_id=partner, device_id_type=MESH)
+
+    for copy in (lines_in, first_in, last_in, reg_in):
         copy.start()
     local_copies = [
         pltpu.make_async_copy(maps_hbm.at[:, 0], local_maps, local_sem.at[0]),
@@ -172,6 +174,12 @@
             high, low = split(value)
             table_hi[row : row + YP, column : column + 128] = high
             table_lo[row : row + YP, column : column + 128] = low
+        for row, column, value in (
+            (0, 0, cosine), (128, 0, -sine), (0, YP, sine), (128, YP, cosine),
+        ):
+            high, low = split(jnp.transpose(value))
+            back_hi[row : row + 128, column : column + YP] = high
+            back_lo[row : row + 128, column : column + YP] = low
         pick[...] = jnp.where(inside & (position == line), 1.0, 0.0).astype(BF16)
 
     phase_tables()
@@ -203,7 +211,7 @@
         for plane in (kspace_re, kspace_im):
             high, low = split(plane)
             spectrum.append(dot(high, pick[...]) + dot(low, pick[...]))
-        field = dot3(jnp.concatenate(spectrum, axis=1), table_hi, table_lo, dot_t)
+        field = dot3(jnp.concatenate(spectrum, axis=1), back_hi, back_lo, dot)
         planes[...] = field
         s_re, s_im = load_planes(lambda group, x: local_maps[group // 8, (group % 8) * XB + x])
         energy = s_re * s_re + s_im * s_im
@@ -512,7 +520,7 @@
         return dot3(weighted, table_hi, table_lo, dot)
 
     def gram_map(vector):
-        planes[...] = dot3(spectrum_of(vector), table_hi, table_lo, dot_t)
+        planes[...] = dot3(spectrum_of(vector), back_hi, back_lo, dot)
         m_re, m_im = maps_re[...], maps_im[...]
         f_re, f_im = planes[:, 0:YP], planes[:, YP : 2 * YP]
         real = jnp.sum((m_re * f_re + m_im * f_im).reshape(16, 8, YP), axis=0)
@@ -624,6 +632,8 @@
             pltpu.VMEM((3, 6, Y, 128), BF16),
             pltpu.VMEM((2 * YP, 256), BF16),
             pltpu.VMEM((2 * YP, 256), BF16),
+            pltpu.VMEM((256, 2 * YP), BF16),
+            pltpu.VMEM((256, 2 * YP), BF16),
             pltpu.VMEM((YP, 128), BF16),
             pltpu.VMEM((CL, XW, 2, Y), F32),
             pltpu.VMEM((CL, XW, 2, Y), F32),

time: 49.6 us -> 49.7 us (level)
  no operation moved by 1% of the time
where the time goes in v8:
time: 49.7 us; the launch traced here: 48.7 us
  Pallas kernels  46.2 us (93%)
  between operations  1.29 us (3%)
  local copies, waits for them, and re-layouts  1.2 us (2%)
    pallas_call x1, Pallas kernels, local(): pl.pallas_call(kernel, out_shape=(block, block), in_specs=[anywhere] * 8,...  46.2 us
    unnamed x2, local copies, waits for them, and re-layouts  1.2 us

profile of v8, /device:TPU:1, one launch (start us, length us, event | category | flops | bytes accessed | tf_op | source)
XLA Modules:
  0.0 48.7 jit_solution(6899116601623716273)
XLA Ops:
  1.3 46.2 %shard_map.95 = (f32[1,4,2,320]{3,2,1,0:T(2,128)S(1)}, f32[1,4,2,320]{3,2,1,0:T(2,128)S(1)}) custom-call(f32[1,4,2,320]{3,2,1,0:T(2,128)} %image_hbm.1, s32[1,80]{1,0:T(1,128)} %lines_hbm.1, f32[4,1,32,2,320]{4,3,2,1,0:T(2,128)} %maps_hbm.1, f32[4,1,32,2,320]{4,3,2,1,0:T(2,128)} %kspace_hbm.1, f32[1]{0:T(128)S(6)} %copy.14.reg_hbm, ...), custom_call_target="tpu_custom_call" | custom-call | tf_op jit(solution)/shard_map/pallas_call | solution.py:608
  47.5 0.6 %copy.12 = f32[1,4,2,320]{3,2,1,0:T(2,128)} copy(f32[1,4,2,320]{3,2,1,0:T(2,128)S(1)} %get-tuple-element.2) | data formatting | bytes 20480
  48.1 0.6 %copy.13 = f32[1,4,2,320]{3,2,1,0:T(2,128)} copy(f32[1,4,2,320]{3,2,1,0:T(2,128)S(1)} %get-tuple-element.3) | data formatting | bytes 20480

commit v9 on v8

--- a/solution.py
+++ b/solution.py
@@ -508,10 +508,6 @@
         jnp.where(first_rows, adjoint, other) + reg * den_re,
         jnp.where(first_rows, other, adjoint) + reg * den_im,
     )
-    energy = finish_stage(0, 2, energy_copies)
-
-    mean = jnp.sum(energy, axis=1, keepdims=True) * (NS / Y / (Z * XW * Y))
-
     def spectrum_of(vector):
         v_re = jnp.broadcast_to(vector[0][None], (16, 8, YP)).reshape(128, YP)
         v_im = jnp.broadcast_to(vector[1][None], (16, 8, YP)).reshape(128, YP)
@@ -534,11 +530,15 @@
 
     pairs = [(i, j) for i in range(4) for j in range(i, 4)]
     basis = [right]
+    first_mapped = gram_map(right)
+    energy = finish_stage(0, 2, energy_copies)
+
+    mean = jnp.sum(energy, axis=1, keepdims=True) * (NS / Y / (Z * XW * Y))
 
     def phase_krylov():
         del basis[1:]
-        for _ in range(3):
-            mapped = gram_map(basis[-1])
+        for step in range(3):
+            mapped = gram_map(basis[-1]) if step else first_mapped
             basis.append((mapped[0] - mean * basis[-1][0], mapped[1] - mean * basis[-1][1]))
         last_spectrum = spectrum_of(basis[-1])
         last_energy = jnp.sum((last_spectrum * last_spectrum).reshape(16, 8, 256), axis=0)

time: 49.7 us -> 49.8 us (level)
  no operation moved by 1% of the time
where the time goes in v9:
time: 49.8 us; the launch traced here: 48.8 us
  Pallas kernels  46.3 us (93%)
  between operations  1.29 us (3%)
  local copies, waits for them, and re-layouts  1.2 us (2%)
    pallas_call x1, Pallas kernels, local(): pl.pallas_call(kernel, out_shape=(block, block), in_specs=[anywhere] * 8,...  46.3 us
    unnamed x2, local copies, waits for them, and re-layouts  1.2 us

profile of v9, /device:TPU:1, one launch (start us, length us, event | category | flops | bytes accessed | tf_op | source)
XLA Modules:
  0.0 48.8 jit_solution(14388396812427940820)
XLA Ops:
  1.3 46.3 %shard_map.95 = (f32[1,4,2,320]{3,2,1,0:T(2,128)S(1)}, f32[1,4,2,320]{3,2,1,0:T(2,128)S(1)}) custom-call(f32[1,4,2,320]{3,2,1,0:T(2,128)} %image_hbm.1, s32[1,80]{1,0:T(1,128)} %lines_hbm.1, f32[4,1,32,2,320]{4,3,2,1,0:T(2,128)} %maps_hbm.1, f32[4,1,32,2,320]{4,3,2,1,0:T(2,128)} %kspace_hbm.1, f32[1]{0:T(128)S(6)} %copy.14.reg_hbm, ...), custom_call_target="tpu_custom_call" | custom-call | tf_op jit(solution)/shard_map/pallas_call | solution.py:608
  47.6 0.6 %copy.12 = f32[1,4,2,320]{3,2,1,0:T(2,128)} copy(f32[1,4,2,320]{3,2,1,0:T(2,128)S(1)} %get-tuple-element.2) | data formatting | bytes 20480
  48.2 0.6 %copy.13 = f32[1,4,2,320]{3,2,1,0:T(2,128)} copy(f32[1,4,2,320]{3,2,1,0:T(2,128)S(1)} %get-tuple-element.3) | data formatting | bytes 20480
